TPU v7x, 32 devices: a whole 2x2x4 slice. The times are simulated.
32 devices in a mesh: ctx: 16 (over z, x, core), tp: 2 (over y).
Axes of the slice: x: 2, y: 2, z: 4, core: 2. Of those that a mesh axis runs over, the one named last changes fastest.
Arguments:
- queries: bfloat16 [4096, 8192], P('ctx', 'tp'), may hold values from -6 to 6
- key_vectors: bfloat16 [4096, 1024], P(('ctx', 'tp')), may hold values from -6 to 6
- value_vectors: bfloat16 [4096, 1024], P(('ctx', 'tp')), may hold values from -6 to 6
- output_gradient: bfloat16 [4096, 8192], P('ctx', 'tp'), may hold values from -6 to 6
- doc_lengths: int32 [8], replicated, may hold values from 1 to 1793, 4096 in all
Outputs:
- attn_output: bfloat16 [4096, 8192], P('ctx', 'tp')
- grad_queries: bfloat16 [4096, 8192], P('ctx', 'tp')
- key_gradient: bfloat16 [4096, 1024], P(('ctx', 'tp'))
- value_gradient: bfloat16 [4096, 1024], P(('ctx', 'tp'))
All inputs are finite; a program needn't handle non-finite values.
Results may differ from a plain program's by a relative error of at most 0.02.
Values may be sent and summed in bfloat16 or wider, within the bound.
No kernel may reach another device: no remote copies, remote signals or barrier semaphores. Data moves between devices by JAX's collectives and lax.ppermute only.
A program may use at most 128 MiB of HBM per device.

v0:
```python
import functools
import math

import jax
import jax.numpy as jnp
from jax import lax
from jax.experimental import pallas as pl
from jax.experimental.pallas import tpu as pltpu
from jax.sharding import PartitionSpec as P

HEAD_SIZE = 128
WINDOW = 8
HEADS_AT_ONCE = 4
SCORE_SCALE = 1.0 / math.sqrt(HEAD_SIZE)
LOG2E = math.log2(math.e)
MASKED = -1e30


def dot(a, b):
    return jnp.dot(a, b, preferred_element_type=jnp.float32)


def group_kernel(heads, unread, own, doc_lengths, q_ref, g_ref, own_ref, far_ref, x_ref, c_ref, *rest):
    out_ref, dq_ref, even_ref, odd_ref, *scratch = rest[unread:]
    (
        q_all, q_turned, g_all, g_turned, k_win, v_win, k_turned, v_turned,
        bias, scores, weights, grads, highest, summed, delta, dq_acc,
    ) = scratch
    rows = q_ref.shape[0]
    at_once = min(heads, HEADS_AT_ONCE)
    repeats = 2 * rows // HEAD_SIZE
    first = own[0] * rows
    doc_start = 0
    start = 0
    for doc in range(doc_lengths.shape[0]):
        doc_start = jnp.where(first >= start, start, doc_start)
        start = start + doc_lengths[doc]
    needed = jnp.clip(own[0] - doc_start // rows + 1, 1, WINDOW)
    trips = (needed + 1) // 2
    spans = [slice(head * rows, (head + 1) * rows) for head in range(heads)]
    columns = [slice(head * HEAD_SIZE, (head + 1) * HEAD_SIZE) for head in range(heads)]
    batches = [slice(head * rows, (head + at_once) * rows) for head in range(0, heads, at_once)]

    for span, column in zip(spans, columns):
        q_all[span, :] = q_ref[:, column]
        q_turned[:, span] = q_ref[:, column].T
    window_refs = [
        own_ref, c_ref.at[0], x_ref.at[0], c_ref.at[1], far_ref, c_ref.at[2], x_ref.at[1], c_ref.at[3]
    ]
    for offset, source in enumerate(window_refs):
        pair, here = offset // 2, slice(offset % 2 * rows, (offset % 2 + 1) * rows)
        k_win[pair, here, :] = source[0]
        v_win[pair, here, :HEAD_SIZE] = source[1]
        v_win[pair, here, HEAD_SIZE:] = jnp.ones((rows, HEAD_SIZE), jnp.bfloat16)
        k_turned[pair, :, here] = source[0].T
        v_turned[pair, :, here] = source[1].T
    query_pos = first + lax.broadcasted_iota(jnp.int32, (rows, HEAD_SIZE), 0)
    low = jnp.zeros((rows, HEAD_SIZE), jnp.int32)
    start = 0
    for doc in range(doc_lengths.shape[0]):
        low = jnp.where(query_pos >= start, start, low)
        start = start + doc_lengths[doc]
    highest[...] = jnp.full(highest.shape, 2 * MASKED, jnp.float32)
    summed[...] = jnp.zeros_like(summed)
    dq_acc[...] = jnp.zeros_like(dq_acc)

    def score_pair(pair, carry):
        for place in range(repeats):
            offset = 2 * pair + place // (repeats // 2)
            key_pos = (
                first - offset * rows + place % (repeats // 2) * HEAD_SIZE
                + lax.broadcasted_iota(jnp.int32, (rows, HEAD_SIZE), 1)
            )
            allowed = (key_pos >= low) & (key_pos <= query_pos)
            bias[:, place * HEAD_SIZE : (place + 1) * HEAD_SIZE] = jnp.where(allowed, 0.0, MASKED)
        for batch in batches:
            part = dot(q_all[batch, :], k_turned[pair])
            for head in range(at_once):
                here = slice(batch.start + head * rows, batch.start + (head + 1) * rows)
                piece = part[head * rows : (head + 1) * rows] * (SCORE_SCALE * LOG2E) + bias[...]
                scores[pair, here, :] = piece
                most = highest[here, :]
                for place in range(repeats):
                    most = jnp.maximum(most, piece[:, place * HEAD_SIZE : (place + 1) * HEAD_SIZE])
                highest[here, :] = most
        return carry

    lax.fori_loop(0, trips, score_pair, 0)
    for span in spans:
        highest[span, :] = jnp.broadcast_to(jnp.max(highest[span, :], axis=1, keepdims=True), (rows, HEAD_SIZE))

    def sum_pair(pair, carry):
        for batch in batches:
            for head in range(at_once):
                here = slice(batch.start + head * rows, batch.start + (head + 1) * rows)
                top = jnp.concatenate([highest[here, :]] * repeats, axis=1)
                weights[pair, here, :] = jnp.exp2(scores[pair, here, :] - top).astype(jnp.bfloat16)
            summed[batch, :] += dot(weights[pair, batch, :], v_win[pair])
        return carry

    lax.fori_loop(0, trips, sum_pair, 0)
    ones = jnp.ones((2 * HEAD_SIZE, HEAD_SIZE), jnp.bfloat16)
    for span, column in zip(spans, columns):
        inverse = 1.0 / summed[span, HEAD_SIZE:]
        output = (summed[span, :HEAD_SIZE] * inverse).astype(jnp.bfloat16)
        out_ref[:, column] = output
        scaled = (g_ref[:, column].astype(jnp.float32) * inverse).astype(jnp.bfloat16)
        g_all[span, :] = scaled
        g_turned[:, span] = scaled.T
        terms = output.astype(jnp.float32) * scaled.astype(jnp.float32)
        upper = terms.astype(jnp.bfloat16)
        lower = (terms - upper.astype(jnp.float32)).astype(jnp.bfloat16)
        delta[span, :] = dot(jnp.concatenate([upper, lower], axis=1), ones)

    def grad_pair(pair, carry):
        for batch in batches:
            part = dot(g_all[batch, :], v_turned[pair])
            for head in range(at_once):
                here = slice(batch.start + head * rows, batch.start + (head + 1) * rows)
                piece = part[head * rows : (head + 1) * rows] - jnp.concatenate([delta[here, :]] * repeats, axis=1)
                grads[here, :] = (weights[pair, here, :].astype(jnp.float32) * piece).astype(jnp.bfloat16)
            dq_acc[batch, :] += dot(grads[batch, :], k_win[pair])
        dk = (dot(q_turned[...], grads[...]) * SCORE_SCALE).astype(jnp.bfloat16)
        dv = dot(g_turned[...], weights[pair]).astype(jnp.bfloat16)
        even_ref[pair, 0] = dk[:, :rows]
        even_ref[pair, 1] = dv[:, :rows]
        odd_ref[pair, 0] = dk[:, rows:]
        odd_ref[pair, 1] = dv[:, rows:]
        return carry

    lax.fori_loop(0, trips, grad_pair, 0)
    for pair in range(WINDOW // 2):

        @pl.when(pair >= trips)
        def _(pair=pair):
            even_ref[pair] = jnp.zeros(even_ref.shape[1:], jnp.bfloat16)
            odd_ref[pair] = jnp.zeros(odd_ref.shape[1:], jnp.bfloat16)

    for span, column in zip(spans, columns):
        dq_ref[:, column] = (dq_acc[span, :] * SCORE_SCALE).astype(jnp.bfloat16)


def attend_group(group, groups, own, doc_lengths, queries, gradient, window, place, buffers, before):
    rows, width = queries.shape
    columns = width // groups
    heads = columns // HEAD_SIZE
    keys = WINDOW * rows
    stacked = heads * rows
    half = WINDOW // 2
    block = pl.BlockSpec((rows, columns), lambda i, *_: (0, group))
    shard = pl.BlockSpec((2, rows, HEAD_SIZE), lambda i, *_: (0, 0, place))
    several = lambda number: pl.BlockSpec((number, 2, rows, HEAD_SIZE), lambda i, *_: (0, 0, 0, place))
    grads_block = pl.BlockSpec((half, 2, HEAD_SIZE, rows), lambda i, *_: (0, 0, 0, 0))
    grads = jax.ShapeDtypeStruct((half, 2, HEAD_SIZE, rows), jnp.bfloat16)
    unread = len(buffers) + len(before)
    short = lambda *shape: pltpu.VMEM(shape, jnp.bfloat16)
    full = lambda *shape: pltpu.VMEM(shape, jnp.float32)
    return pl.pallas_call(
        functools.partial(group_kernel, heads, unread),
        grid_spec=pltpu.PrefetchScalarGridSpec(
            num_scalar_prefetch=2,
            grid=(1,),
            in_specs=[block, block, shard, shard, several(half // 2), several(half)]
            + [pl.BlockSpec(memory_space=pl.ANY)] * unread,
            out_specs=[block, block, grads_block, grads_block],
            scratch_shapes=[
                short(stacked, HEAD_SIZE),
                short(HEAD_SIZE, stacked),
                short(stacked, HEAD_SIZE),
                short(HEAD_SIZE, stacked),
                short(half, 2 * rows, HEAD_SIZE),
                short(half, 2 * rows, 2 * HEAD_SIZE),
                short(half, HEAD_SIZE, 2 * rows),
                short(half, HEAD_SIZE, 2 * rows),
                full(rows, 2 * rows),
                full(half, stacked, 2 * rows),
                short(half, stacked, 2 * rows),
                short(stacked, 2 * rows),
                full(stacked, HEAD_SIZE),
                full(stacked, 2 * HEAD_SIZE),
                full(stacked, HEAD_SIZE),
                full(stacked, HEAD_SIZE),
            ],
        ),
        out_shape=[
            jax.ShapeDtypeStruct(queries.shape, jnp.bfloat16),
            jax.ShapeDtypeStruct(queries.shape, jnp.bfloat16),
            grads,
            grads,
        ],
        input_output_aliases={8 + number: number for number in range(len(buffers))},
        compiler_params=pltpu.CompilerParams(vmem_limit_bytes=56 * 1024 * 1024),
        cost_estimate=pl.CostEstimate(
            flops=4 * 6 * 2 * heads * rows * keys * HEAD_SIZE,
            bytes_accessed=8 * rows * columns + 8 * keys * HEAD_SIZE,
            transcendentals=heads * rows * keys,
        ),
        name=f"attend_group_{group}",
    )(own, doc_lengths, queries, gradient, *window, *buffers, *before)


def shifted(value, steps):
    count = lax.axis_size("ctx")
    sources = range(max(0, -steps), min(count, count - steps))
    return lax.ppermute(value, "ctx", [(source, source + steps) for source in sources])


def swapped(value, bit):
    return lax.ppermute(value, "ctx", [(place, place ^ bit) for place in range(lax.axis_size("ctx"))])


def tp_received(block_for):
    count = lax.axis_size("tp")
    own = lax.axis_index("tp")
    received = []
    for step in range(1, count):
        sent = block_for(lax.rem(own + step, count), step)
        received.append(lax.ppermute(sent, "tp", [(place, (place + step) % count) for place in range(count)]))
    return received


def in_tp_order(mine, received):
    count = lax.axis_size("tp")
    own = lax.axis_index("tp")
    parts = [mine, *received]
    ordered = []
    for place in range(count):
        part = parts[0]
        for step in range(1, count):
            part = jnp.where(lax.rem(own - step + count, count) == place, parts[step], part)
        ordered.append(part)
    return ordered


def whole_block(shape):
    return pl.BlockSpec(shape, lambda i, *_: (0,) * len(shape))


def small_kernel(kernel, scalars, operands, specs, outs, before, name):
    return pl.pallas_call(
        kernel,
        grid_spec=pltpu.PrefetchScalarGridSpec(
            num_scalar_prefetch=1,
            grid=(1,),
            in_specs=specs + [pl.BlockSpec(memory_space=pl.ANY)] * len(before),
            out_specs=[whole_block(shape) for shape in outs],
        ),
        out_shape=[jax.ShapeDtypeStruct(shape, jnp.bfloat16) for shape in outs],
        compiler_params=pltpu.CompilerParams(vmem_limit_bytes=32 * 1024 * 1024),
        name=name,
    )(scalars, *operands, *before)


def pack_for_tp(key_vectors, value_vectors, groups, tp_own):
    count = lax.axis_size("tp")
    local = key_vectors.shape[0]
    columns = groups * HEAD_SIZE
    blocks = [
        pl.BlockSpec((local, columns), lambda i, own, step=step: (0, lax.rem(own[0] + step, count)))
        for step in range(1, count)
    ]

    def kernel(own, *refs):
        keys, values, outs = refs[: count - 1], refs[count - 1 : 2 * count - 2], refs[1 - count :]
        for key, value, out in zip(keys, values, outs):
            out[0] = key[...]
            out[1] = value[...]

    return small_kernel(
        kernel, tp_own, [key_vectors] * (count - 1) + [value_vectors] * (count - 1), blocks + blocks,
        [(2, local, columns)] * (count - 1), [], "pack_for_tp",
    )


def join_tokens(key_vectors, value_vectors, received, groups, bounds, tp_own):
    count = lax.axis_size("tp")
    local = key_vectors.shape[0]
    block = pl.BlockSpec((local, groups * HEAD_SIZE), lambda i, own: (0, own[0]))

    def kernel(own, key, value, *refs):
        parts, outs = refs[: count - 1], refs[count - 1 :]
        for (first, last), out in zip(bounds, outs):
            columns = slice(first * HEAD_SIZE, last * HEAD_SIZE)
            here = pl.ds(pl.multiple_of(own[0] * local, local), local)
            out[0, here, :] = key[:, columns]
            out[1, here, :] = value[:, columns]
            for step in range(1, count):
                source = lax.rem(own[0] - step + count, count)
                rows = pl.ds(pl.multiple_of(source * local, local), local)
                out[:, rows, :] = parts[step - 1][:, :, columns]

    return small_kernel(
        kernel, tp_own, [key_vectors, value_vectors, *received],
        [block, block] + [whole_block(part.shape) for part in received],
        [(2, local * count, (last - first) * HEAD_SIZE) for first, last in bounds], [], "join_tokens",
    )


def even_window(own_pair, own):
    far = shifted(own_pair, WINDOW // 2)
    beyond = shifted(far, WINDOW // 2)
    low_x = (own // 2) % 2 == 0
    x_sent = jnp.stack([jnp.where(low_x, own_pair, far), jnp.where(low_x, far, beyond)])
    return own_pair, far, beyond, x_sent


def whole_window(evens, own, before, name):
    own_pair, far, beyond, x_sent = evens
    x_pairs = swapped(x_sent, 2)
    half = WINDOW // 2

    def kernel(own, own_ref, far_ref, beyond_ref, x_ref, *refs):
        out = refs[-1]
        evens = [own_ref, x_ref.at[0], far_ref, x_ref.at[1], beyond_ref]
        low_c = lax.rem(own[0], 2)
        for bit in range(2):

            @pl.when(low_c == bit)
            def _(bit=bit):
                for place in range(half):
                    out[place] = evens[place + bit][...]

    operands = [own_pair, far, beyond, x_pairs]
    (c_sent,) = small_kernel(
        kernel, own, operands, [whole_block(part.shape) for part in operands],
        [(half, *own_pair.shape)], before, name,
    )
    return own_pair, far, x_pairs, swapped(c_sent, 1)


def wide(part):
    return part.astype(jnp.float32)


def fold_cores(even, got, own, before, name):
    half = WINDOW // 2

    def kernel(own, even_ref, got_ref, *refs):
        sent, kept = refs[-2:]
        for bit in range(2):

            @pl.when(lax.rem(own[0], 2) == bit)
            def _(bit=bit):
                for place in range(half + 1):
                    out = sent.at[place // 2] if place % 2 else kept.at[place // 2]
                    total = None
                    if place < half:
                        total = wide(even_ref[place])
                    if 0 <= place - bit < half:
                        more = wide(got_ref[place - bit])
                        total = more if total is None else total + more
                    out[...] = jnp.zeros(out.shape, out.dtype) if total is None else total.astype(out.dtype)

    shape = even.shape[1:]
    return small_kernel(
        kernel, own, [even, got], [whole_block(even.shape)] * 2,
        [(half // 2, *shape), (half // 2 + 1, *shape)], before, name,
    )


def fold_x(sent, kept, own, before, name):
    got = swapped(sent, 2)

    def kernel(own, kept_ref, got_ref, *refs):
        near, far, beyond = refs[-3:]
        for bit in range(2):

            @pl.when(lax.rem(own[0] // 2, 2) == bit)
            def _(bit=bit):
                for place, out in enumerate((near, far, beyond)):
                    total = wide(kept_ref[place])
                    if 0 <= place - bit < got_ref.shape[0]:
                        total = total + wide(got_ref[place - bit])
                    out[...] = total.astype(out.dtype)

    return small_kernel(
        kernel, own, [kept, got], [whole_block(kept.shape), whole_block(got.shape)], [kept.shape[1:]] * 3, before, name
    )


def body(queries, key_vectors, value_vectors, output_gradient, doc_lengths):
    own = lax.axis_index("ctx")
    own_info = own.reshape(1).astype(jnp.int32)
    local = key_vectors.shape[0]
    all_groups = key_vectors.shape[1] // HEAD_SIZE
    tp_count = lax.axis_size("tp")
    groups = all_groups // tp_count
    tp_own = lax.axis_index("tp")
    tp_info = tp_own.reshape(1).astype(jnp.int32)

    bounds = [(0, 1)] + ([(1, groups)] if groups > 1 else [])
    packed = pack_for_tp(key_vectors, value_vectors, groups, tp_info)
    received = tp_received(lambda place, step: packed[step - 1])
    chunks = join_tokens(key_vectors, value_vectors, received, groups, bounds, tp_info)
    evens = [even_window(chunk, own) for chunk in chunks]

    windows = [whole_window(evens[0], own_info, [], "core_swap_0")]
    buffers = ()
    results, got, folded, sums = [], [], [], []

    def fold_next_cores(before):
        group = len(folded)
        folded.append(fold_cores(results[group][2], got[group], own_info, before, f"fold_cores_{group}"))

    def fold_next_x(before):
        group = len(sums)
        sums.append(fold_x(*folded[group], own_info, before, f"fold_x_{group}"))

    for group in range(groups):
        waits = [evens[1][3]] if group == 0 and groups > 1 else []
        if group >= 2:
            waits.append(folded[group - 2][0])
        if group >= 3:
            waits.append(sums[group - 3][1])
        chunk = min(group, 1)
        results.append(
            attend_group(
                group, groups, own_info, doc_lengths, queries, output_gradient, windows[chunk], group - chunk,
                buffers, waits,
            )
        )
        *buffers, even, odd = results[-1]
        got.append(swapped(odd, 1))
        if group == 0 and groups > 1:
            windows.append(whole_window(evens[1], own_info, [even], "core_swap_1"))
        if group >= 1:
            fold_next_cores([even])
        if group >= 2 and group < groups - 1:
            fold_next_x([even])
    while len(sums) < groups - 2:
        fold_next_x([got[-1]])
    fold_next_cores([])
    while len(sums) < groups:
        fold_next_x([folded[-1][0]] if len(sums) < groups - 1 else [])

    totals = []
    for near, far, beyond in sums:
        total = wide(near) + wide(shifted(beyond, -WINDOW)) + wide(shifted(far, -(WINDOW // 2)))
        totals.append(jnp.swapaxes(total.astype(jnp.bfloat16), 1, 2))

    def exchanged(total):
        def tokens_of(place, step=0):
            return lax.dynamic_slice_in_dim(total, place * local, local, total.ndim - 2)

        return in_tp_order(tokens_of(tp_own), tp_received(tokens_of))

    if groups > 1:
        early = exchanged(jnp.stack(totals[:-1]))
        late = exchanged(totals[-1])
        ordered = [[*(part[group] for group in range(groups - 1)), last] for part, last in zip(early, late)]
    else:
        ordered = [[part] for part in exchanged(totals[0])]

    def output(which):
        return jnp.concatenate([part[which] for source in ordered for part in source], axis=1)

    out, dq = buffers
    return out, dq, output(0), output(1)


def solution(mesh):
    tokens = P(("ctx", "tp"), None)
    heads = P("ctx", "tp")
    return jax.shard_map(
        body,
        mesh=mesh,
        in_specs=(heads, tokens, tokens, heads, P()),
        out_specs=(heads, heads, tokens, tokens),
        check_vma=False,
    )
```

profile of v0, /device:TPU:18, one launch (start us, length us, event | category | flops | bytes accessed | tf_op | source)
XLA Modules:
  0.0 174.0 jit_solution(11922772547882619838)
XLA Ops:
  0.6 0.9 copy-done.11
  1.6 0.9 copy-done.12
  2.6 1.6 collective-permute-start
  4.1 6.5 %collective-permute-done.refs_0_ = bf16[2,128,512]{2,1,0:T(8,128)(2,1)S(1)} collective-permute-done((bf16[2,128,512]{2,1,0:T(8,128)(2,1)S(1)}, bf16[2,128,512]{2,1,0:T(8,128)(2,1)S(1)}, u32[]{:S(2)}, u32[]{:S(2)}) %collective-permute-start) | collective-permute-done | bytes 262176 | tf_op jit(solution)/shard_map/ppermute | solution.py:218
  10.8 3.5 %collective-permute-start.4 = (bf16[2,256,128]{2,1,0:T(8,128)(2,1)S(1)}, bf16[2,256,128]{2,1,0:T(8,128)(2,1)S(1)}, u32[]{:S(2)}, u32[]{:S(2)}) collective-permute-start(bf16[2,256,128]{2,1,0:T(8,128)(2,1)S(1)} %get-tuple-element.43.own_ref), channel_id=1, source_target_pairs={{0,8},{2,10},{4,12},{6,14},{8,16},{10,18},{12,20},{14,22},{16,24},... | collective-permute-start | bytes 393224 | tf_op jit(solution)/shard_map/ppermute | solution.py:205
  14.3 1.9 %collective-permute-start.1 = (bf16[2,256,384]{2,1,0:T(8,128)(2,1)S(1)}, bf16[2,256,384]{2,1,0:T(8,128)(2,1)S(1)}, u32[]{:S(2)}, u32[]{:S(2)}) collective-permute-start(bf16[2,256,384]{2,1,0:T(8,128)(2,1)S(1)} %get-tuple-element.42.own_ref), channel_id=1, source_target_pairs={{0,8},{2,10},{4,12},{6,14},{8,16},{10,18},{12,20},{14,22},{16,24},... | collective-permute-start | bytes 1179656 | tf_op jit(solution)/shard_map/ppermute | solution.py:205
  16.2 1.9 %collective-permute-done.4.far_ref = bf16[2,256,128]{2,1,0:T(8,128)(2,1)S(1)} collective-permute-done((bf16[2,256,128]{2,1,0:T(8,128)(2,1)S(1)}, bf16[2,256,128]{2,1,0:T(8,128)(2,1)S(1)}, u32[]{:S(2)}, u32[]{:S(2)}) %collective-permute-start.4) | collective-permute-done | bytes 131104 | tf_op jit(solution)/shard_map/ppermute | solution.py:205
  18.1 4.4 %collective-permute-start.5 = (bf16[2,256,128]{2,1,0:T(8,128)(2,1)S(1)}, bf16[2,256,128]{2,1,0:T(8,128)(2,1)S(1)}, u32[]{:S(2)}, u32[]{:S(2)}) collective-permute-start(bf16[2,256,128]{2,1,0:T(8,128)(2,1)S(1)} %collective-permute-done.4.far_ref), channel_id=1, source_target_pairs={{0,8},{2,10},{4,12},{6,14},{8,16},{10,18},{12,20},{14,22},{16,24},... | collective-permute-start | bytes 393224 | tf_op jit(solution)/shard_map/ppermute | solution.py:205
  22.5 6.3 %collective-permute-done.5.beyond_ref = bf16[2,256,128]{2,1,0:T(8,128)(2,1)S(1)} collective-permute-done((bf16[2,256,128]{2,1,0:T(8,128)(2,1)S(1)}, bf16[2,256,128]{2,1,0:T(8,128)(2,1)S(1)}, u32[]{:S(2)}, u32[]{:S(2)}) %collective-permute-start.5) | collective-permute-done | bytes 131104 | tf_op jit(solution)/shard_map/ppermute | solution.py:205
  28.9 3.4 %collective-permute-start.2 = (bf16[2,256,384]{2,1,0:T(8,128)(2,1)S(1)}, bf16[2,256,384]{2,1,0:T(8,128)(2,1)S(1)}, u32[]{:S(2)}, u32[]{:S(2)}) collective-permute-start(bf16[2,256,384]{2,1,0:T(8,128)(2,1)S(1)} %collective-permute-done.1.far_ref), channel_id=1, source_target_pairs={{0,8},{2,10},{4,12},{6,14},{8,16},{10,18},{12,20},{14,22},{16,24},... | collective-permute-start | bytes 1179656 | tf_op jit(solution)/shard_map/ppermute | solution.py:205
  33.0 6.0 %collective-permute-done.6.x_ref = bf16[2,2,256,128]{3,2,1,0:T(8,128)(2,1)S(1)} collective-permute-done((bf16[2,2,256,128]{3,2,1,0:T(8,128)(2,1)S(1)}, bf16[2,2,256,128]{3,2,1,0:T(8,128)(2,1)S(1)}, u32[]{:S(2)}, u32[]{:S(2)}) %collective-permute-start.6) | collective-permute-done | bytes 262176 | tf_op jit(solution)/shard_map/ppermute | solution.py:209
  39.1 0.7 collective-permute-done.2.beyond_ref
  41.0 0.8 copy-done.25
  41.8 8.9 %attend_group_0.1 = (bf16[256,4096]{1,0:T(8,128)(2,1)}, bf16[256,4096]{1,0:T(8,128)(2,1)}, bf16[4,2,128,256]{3,2,1,0:T(8,128)(2,1)}, bf16[4,2,128,256]{3,2,1,0:T(8,128)(2,1)}) custom-call(s32[1]{0:T(128)} %bitcast.own, s32[8]{0:T(128)} %doc_lengths.7, bf16[256,4096]{1,0:T(8,128)(2,1)} %q_ref.7, bf16[256,4096]{1,0:T(8,128)(2,1)} %g_ref.7, ...), custom_call_target="tpu_custom_call" | custom-call | flops 25769803776 | bytes 4194304 | tf_op jit(solution)/shard_map/attend_group_0/pallas_call | solution.py:158
  50.7 8.6 %collective-permute-done.3.x_ref = bf16[2,2,256,384]{3,2,1,0:T(8,128)(2,1)S(1)} collective-permute-done((bf16[2,2,256,384]{3,2,1,0:T(8,128)(2,1)S(1)}, bf16[2,2,256,384]{3,2,1,0:T(8,128)(2,1)S(1)}, u32[]{:S(2)}, u32[]{:S(2)}) %collective-permute-start.3) | collective-permute-done | bytes 786464 | tf_op jit(solution)/shard_map/ppermute | solution.py:209
  59.4 1.3 copy-done.3
  60.9 0.8 copy-done.24
  61.7 2.6 %collective-permute-done.8.c_ref = bf16[4,2,256,384]{3,2,1,0:T(8,128)(2,1)S(1)} collective-permute-done((bf16[4,2,256,384]{3,2,1,0:T(8,128)(2,1)S(1)}, bf16[4,2,256,384]{3,2,1,0:T(8,128)(2,1)S(1)}, u32[]{:S(2)}, u32[]{:S(2)}) %collective-permute-start.8) | collective-permute-done | bytes 1572896 | tf_op jit(solution)/shard_map/ppermute | solution.py:209
  64.3 1.2 copy-done.23
  65.5 9.4 %attend_group_1.1 = (bf16[256,4096]{1,0:T(8,128)(2,1)}, bf16[256,4096]{1,0:T(8,128)(2,1)}, bf16[4,2,128,256]{3,2,1,0:T(8,128)(2,1)}, bf16[4,2,128,256]{3,2,1,0:T(8,128)(2,1)}) custom-call(s32[1]{0:T(128)} %bitcast.own, s32[8]{0:T(128)} %doc_lengths.7, bf16[256,4096]{1,0:T(8,128)(2,1)} %q_ref.7, ...), custom_call_target="tpu_custom_call", output_to_operand_aliasing={{0}: (8, {}), {1}: (9, {})} | custom-call | flops 25769803776 | bytes 4194304 | tf_op jit(solution)/shard_map/attend_group_1/pallas_call | solution.py:158
  74.9 1.0 copy-done.7
  76.1 11.8 %collective-permute-start.11 = (bf16[2,2,128,256]{3,2,1,0:T(8,128)(2,1)S(1)}, bf16[2,2,128,256]{3,2,1,0:T(8,128)(2,1)S(1)}, u32[]{:S(2)}, u32[]{:S(2)}) collective-permute-start(bf16[2,2,128,256]{3,2,1,0:T(8,128)(2,1)S(1)} %get-tuple-element.51.rest_2_), channel_id=1, source_target_pairs={{0,4},{2,6},{4,0},{6,2},{8,12},{10,14},{12,8},{14,10},{16,20},{18,... | collective-permute-start | bytes 786440 | tf_op jit(solution)/shard_map/ppermute | solution.py:209
  87.8 9.0 %attend_group_2.1 = (bf16[256,4096]{1,0:T(8,128)(2,1)}, bf16[256,4096]{1,0:T(8,128)(2,1)}, bf16[4,2,128,256]{3,2,1,0:T(8,128)(2,1)}, bf16[4,2,128,256]{3,2,1,0:T(8,128)(2,1)}) custom-call(s32[1]{0:T(128)} %bitcast.own, s32[8]{0:T(128)} %doc_lengths.7, bf16[256,4096]{1,0:T(8,128)(2,1)} %q_ref.7, ...), custom_call_target="tpu_custom_call", output_to_operand_aliasing={{0}: (8, {}), {1}: (9, {})} | custom-call | flops 25769803776 | bytes 4194304 | tf_op jit(solution)/shard_map/attend_group_2/pallas_call | solution.py:158
  97.4 1.0 copy-done
  98.5 0.6 copy-done.20
  99.2 1.0 copy-done.1
  100.4 0.7 copy-done.17
  101.1 9.0 %attend_group_3.1 = (bf16[256,4096]{1,0:T(8,128)(2,1)}, bf16[256,4096]{1,0:T(8,128)(2,1)}, bf16[4,2,128,256]{3,2,1,0:T(8,128)(2,1)}, bf16[4,2,128,256]{3,2,1,0:T(8,128)(2,1)}) custom-call(s32[1]{0:T(128)} %bitcast.own, s32[8]{0:T(128)} %doc_lengths.7, bf16[256,4096]{1,0:T(8,128)(2,1)} %q_ref.7, ...), custom_call_target="tpu_custom_call", output_to_operand_aliasing={{0}: (8, {}), {1}: (9, {})} | custom-call | flops 25769803776 | bytes 4194304 | tf_op jit(solution)/shard_map/attend_group_3/pallas_call | solution.py:158
  110.1 19.8 %collective-permute-start.14 = (bf16[2,2,128,256]{3,2,1,0:T(8,128)(2,1)S(1)}, bf16[2,2,128,256]{3,2,1,0:T(8,128)(2,1)S(1)}, u32[]{:S(2)}, u32[]{:S(2)}) collective-permute-start(bf16[2,2,128,256]{3,2,1,0:T(8,128)(2,1)S(1)} %copy-done.18), channel_id=1, source_target_pairs={{0,4},{2,6},{4,0},{6,2},{8,12},{10,14},{12,8},{14,10},{16,20},{18,... | collective-permute-start | bytes 786440 | tf_op jit(solution)/shard_map/ppermute | solution.py:209
  129.9 1.3 collective-permute-start.12
  131.2 1.9 %collective-permute-start.13 = (bf16[2,128,256]{2,1,0:T(8,128)(2,1)S(1)}, bf16[2,128,256]{2,1,0:T(8,128)(2,1)S(1)}, u32[]{:S(2)}, u32[]{:S(2)}) collective-permute-start(bf16[2,128,256]{2,1,0:T(8,128)(2,1)S(1)} %copy-done.21), channel_id=1, source_target_pairs={{8,0},{10,2},{12,4},{14,6},{16,8},{18,10},{20,12},{22,14},{24,16},... | collective-permute-start | bytes 393224 | tf_op jit(solution)/shard_map/ppermute | solution.py:205
  133.2 1.0 copy-done.5
  134.4 2.1 %collective-permute-done.14.got_ref = bf16[2,2,128,256]{3,2,1,0:T(8,128)(2,1)S(1)} collective-permute-done((bf16[2,2,128,256]{3,2,1,0:T(8,128)(2,1)S(1)}, bf16[2,2,128,256]{3,2,1,0:T(8,128)(2,1)S(1)}, u32[]{:S(2)}, u32[]{:S(2)}) %collective-permute-start.14) | collective-permute-done | bytes 262176 | tf_op jit(solution)/shard_map/ppermute | solution.py:209
  136.7 1.3 collective-permute-start.16
  138.0 1.9 %collective-permute-start.17 = (bf16[2,128,256]{2,1,0:T(8,128)(2,1)S(1)}, bf16[2,128,256]{2,1,0:T(8,128)(2,1)S(1)}, u32[]{:S(2)}, u32[]{:S(2)}) collective-permute-start(bf16[2,128,256]{2,1,0:T(8,128)(2,1)S(1)} %get-tuple-element.67), channel_id=1, source_target_pairs={{8,0},{10,2},{12,4},{14,6},{16,8},{18,10},{20,12},{22,14},{24,16},... | collective-permute-start | bytes 393224 | tf_op jit(solution)/shard_map/ppermute | solution.py:205
  140.1 2.6 %collective-permute-start.23 = (bf16[2,2,128,256]{3,2,1,0:T(8,128)(2,1)S(1)}, bf16[2,2,128,256]{3,2,1,0:T(8,128)(2,1)S(1)}, u32[]{:S(2)}, u32[]{:S(2)}) collective-permute-start(bf16[2,2,128,256]{3,2,1,0:T(8,128)(2,1)S(1)} %get-tuple-element.72.refs_0_), channel_id=1, source_target_pairs={{0,4},{2,6},{4,0},{6,2},{8,12},{10,14},{12,8},{14,10},{16,20},{18,... | collective-permute-start | bytes 786440 | tf_op jit(solution)/shard_map/ppermute | solution.py:209
  142.8 1.3 collective-permute-start.20
  144.1 1.9 %collective-permute-start.21 = (bf16[2,128,256]{2,1,0:T(8,128)(2,1)S(1)}, bf16[2,128,256]{2,1,0:T(8,128)(2,1)S(1)}, u32[]{:S(2)}, u32[]{:S(2)}) collective-permute-start(bf16[2,128,256]{2,1,0:T(8,128)(2,1)S(1)} %get-tuple-element.75), channel_id=1, source_target_pairs={{8,0},{10,2},{12,4},{14,6},{16,8},{18,10},{20,12},{22,14},{24,16},... | collective-permute-start | bytes 393224 | tf_op jit(solution)/shard_map/ppermute | solution.py:205
  146.0 1.6 collective-permute-done.17
  147.7 3.8 %collective-permute-done.20 = bf16[2,128,256]{2,1,0:T(8,128)(2,1)S(1)} collective-permute-done((bf16[2,128,256]{2,1,0:T(8,128)(2,1)S(1)}, bf16[2,128,256]{2,1,0:T(8,128)(2,1)S(1)}, u32[]{:S(2)}, u32[]{:S(2)}) %collective-permute-start.20) | collective-permute-done | bytes 131104 | tf_op jit(solution)/shard_map/ppermute | solution.py:205
  151.5 2.7 %collective-permute-done.21 = bf16[2,128,256]{2,1,0:T(8,128)(2,1)S(1)} collective-permute-done((bf16[2,128,256]{2,1,0:T(8,128)(2,1)S(1)}, bf16[2,128,256]{2,1,0:T(8,128)(2,1)S(1)}, u32[]{:S(2)}, u32[]{:S(2)}) %collective-permute-start.21) | collective-permute-done | bytes 131104 | tf_op jit(solution)/shard_map/ppermute | solution.py:205
  154.4 1.6 collective-permute-start.22
  156.0 2.6 %collective-permute-start.24 = (bf16[2,128,256]{2,1,0:T(8,128)(2,1)S(1)}, bf16[2,128,256]{2,1,0:T(8,128)(2,1)S(1)}, u32[]{:S(2)}, u32[]{:S(2)}) collective-permute-start(bf16[2,128,256]{2,1,0:T(8,128)(2,1)S(1)} %get-tuple-element.78), channel_id=1, source_target_pairs={{16,0},{18,2},{20,4},{22,6},{24,8},{26,10},{28,12},{30,14},{17,1},... | collective-permute-start | bytes 393224 | tf_op jit(solution)/shard_map/ppermute | solution.py:205
  158.6 3.1 %collective-permute-start.25 = (bf16[2,128,256]{2,1,0:T(8,128)(2,1)S(1)}, bf16[2,128,256]{2,1,0:T(8,128)(2,1)S(1)}, u32[]{:S(2)}, u32[]{:S(2)}) collective-permute-start(bf16[2,128,256]{2,1,0:T(8,128)(2,1)S(1)} %get-tuple-element.79), channel_id=1, source_target_pairs={{8,0},{10,2},{12,4},{14,6},{16,8},{18,10},{20,12},{22,14},{24,16},... | collective-permute-start | bytes 393224 | tf_op jit(solution)/shard_map/ppermute | solution.py:205
  161.9 5.9 %collective-permute-done.25 = bf16[2,128,256]{2,1,0:T(8,128)(2,1)S(1)} collective-permute-done((bf16[2,128,256]{2,1,0:T(8,128)(2,1)S(1)}, bf16[2,128,256]{2,1,0:T(8,128)(2,1)S(1)}, u32[]{:S(2)}, u32[]{:S(2)}) %collective-permute-start.25) | collective-permute-done | bytes 131104 | tf_op jit(solution)/shard_map/ppermute | solution.py:205
  168.5 3.7 %collective-permute-done.26 = bf16[2,128,128]{1,2,0:T(8,128)(2,1)S(1)} collective-permute-done((bf16[2,128,128]{1,2,0:T(8,128)(2,1)S(1)}, bf16[2,128,128]{1,2,0:T(8,128)(2,1)S(1)}, u32[]{:S(2)}, u32[]{:S(2)}) %collective-permute-start.26) | collective-permute-done | bytes 65568 | tf_op jit(solution)/shard_map/ppermute | solution.py:218
  172.3 0.9 copy.15
  173.2 0.8 copy.16
  (97 shorter events, 4.9 us)
Async XLA Ops:
  2.6 8.1 %collective-permute-start = (bf16[2,128,512]{2,1,0:T(8,128)(2,1)S(1)}, bf16[2,128,512]{2,1,0:T(8,128)(2,1)S(1)}, u32[]{:S(2)}, u32[]{:S(2)}) collective-permute-start(bf16[2,128,512]{2,1,0:T(8,128)(2,1)S(1)} %pack_for_tp.1), channel_id=1, source_target_pairs={{0,1},{1,0},{2,3},{3,2},{4,5},{5,4},{6,7},{7,6},{8,9},{9,8},{10,11... | collective-permute-start | bytes 786440 | tf_op jit(solution)/shard_map/ppermute | solution.py:218
  10.7 29.1 %copy-start.14 = (bf16[2,256,128]{2,1,0:T(8,128)(2,1)}, bf16[2,256,128]{2,1,0:T(8,128)(2,1)S(1)}, u32[]{:S(2)}) copy-start(bf16[2,256,128]{2,1,0:T(8,128)(2,1)S(1)} %get-tuple-element.43.own_ref) | copy-start | bytes 393220
  10.8 48.6 %copy-start.9 = (bf16[2,256,384]{2,1,0:T(8,128)(2,1)}, bf16[2,256,384]{2,1,0:T(8,128)(2,1)S(1)}, u32[]{:S(2)}) copy-start(bf16[2,256,384]{2,1,0:T(8,128)(2,1)S(1)} %get-tuple-element.42.own_ref) | copy-start | bytes 1179652
  10.8 7.4 %collective-permute-start.4 = (bf16[2,256,128]{2,1,0:T(8,128)(2,1)S(1)}, bf16[2,256,128]{2,1,0:T(8,128)(2,1)S(1)}, u32[]{:S(2)}, u32[]{:S(2)}) collective-permute-start(bf16[2,256,128]{2,1,0:T(8,128)(2,1)S(1)} %get-tuple-element.43.own_ref), channel_id=1, source_target_pairs={{0,8},{2,10},{4,12},{6,14},{8,16},{10,18},{12,20},{14,22},{16,24},... | collective-permute-start | bytes 393224 | tf_op jit(solution)/shard_map/ppermute | solution.py:205
  14.3 14.6 %collective-permute-start.1 = (bf16[2,256,384]{2,1,0:T(8,128)(2,1)S(1)}, bf16[2,256,384]{2,1,0:T(8,128)(2,1)S(1)}, u32[]{:S(2)}, u32[]{:S(2)}) collective-permute-start(bf16[2,256,384]{2,1,0:T(8,128)(2,1)S(1)} %get-tuple-element.42.own_ref), channel_id=1, source_target_pairs={{0,8},{2,10},{4,12},{6,14},{8,16},{10,18},{12,20},{14,22},{16,24},... | collective-permute-start | bytes 1179656 | tf_op jit(solution)/shard_map/ppermute | solution.py:205
  18.1 21.8 %copy-start.15 = (bf16[2,256,128]{2,1,0:T(8,128)(2,1)}, bf16[2,256,128]{2,1,0:T(8,128)(2,1)S(1)}, u32[]{:S(2)}) copy-start(bf16[2,256,128]{2,1,0:T(8,128)(2,1)S(1)} %collective-permute-done.4.far_ref) | copy-start | bytes 393220
  18.1 10.7 %collective-permute-start.5 = (bf16[2,256,128]{2,1,0:T(8,128)(2,1)S(1)}, bf16[2,256,128]{2,1,0:T(8,128)(2,1)S(1)}, u32[]{:S(2)}, u32[]{:S(2)}) collective-permute-start(bf16[2,256,128]{2,1,0:T(8,128)(2,1)S(1)} %collective-permute-done.4.far_ref), channel_id=1, source_target_pairs={{0,8},{2,10},{4,12},{6,14},{8,16},{10,18},{12,20},{14,22},{16,24},... | collective-permute-start | bytes 393224 | tf_op jit(solution)/shard_map/ppermute | solution.py:205
  28.9 30.4 %copy-start.10 = (bf16[2,256,384]{2,1,0:T(8,128)(2,1)}, bf16[2,256,384]{2,1,0:T(8,128)(2,1)S(1)}, u32[]{:S(2)}) copy-start(bf16[2,256,384]{2,1,0:T(8,128)(2,1)S(1)} %collective-permute-done.1.far_ref) | copy-start | bytes 1179652
  28.9 10.9 %collective-permute-start.2 = (bf16[2,256,384]{2,1,0:T(8,128)(2,1)S(1)}, bf16[2,256,384]{2,1,0:T(8,128)(2,1)S(1)}, u32[]{:S(2)}, u32[]{:S(2)}) collective-permute-start(bf16[2,256,384]{2,1,0:T(8,128)(2,1)S(1)} %collective-permute-done.1.far_ref), channel_id=1, source_target_pairs={{0,8},{2,10},{4,12},{6,14},{8,16},{10,18},{12,20},{14,22},{16,24},... | collective-permute-start | bytes 1179656 | tf_op jit(solution)/shard_map/ppermute | solution.py:205
  32.4 6.6 %collective-permute-start.6 = (bf16[2,2,256,128]{3,2,1,0:T(8,128)(2,1)S(1)}, bf16[2,2,256,128]{3,2,1,0:T(8,128)(2,1)S(1)}, u32[]{:S(2)}, u32[]{:S(2)}) collective-permute-start(bf16[2,2,256,128]{3,2,1,0:T(8,128)(2,1)S(1)} %pad_maximum_fusion.2), channel_id=1, source_target_pairs={{0,4},{2,6},{4,0},{6,2},{8,12},{10,14},{12,8},{14,10},{16,20},{18,... | collective-permute-start | bytes 786440 | tf_op jit(solution)/shard_map/ppermute | solution.py:209
  39.0 1.0 copy-start.16
  39.0 2.0 %collective-permute-start.7 = (bf16[4,2,256,128]{3,2,1,0:T(8,128)(2,1)S(1)}, bf16[4,2,256,128]{3,2,1,0:T(8,128)(2,1)S(1)}, u32[]{:S(2)}, u32[]{:S(2)}) collective-permute-start(bf16[4,2,256,128]{3,2,1,0:T(8,128)(2,1)S(1)} %core_swap_0.1), channel_id=1, source_target_pairs={{0,2},{2,0},{4,6},{6,4},{8,10},{10,8},{12,14},{14,12},{16,18},{18,... | collective-permute-start | bytes 1572872 | tf_op jit(solution)/shard_map/ppermute | solution.py:209
  40.0 1.0 copy-start.22
  40.0 19.3 %collective-permute-start.3 = (bf16[2,2,256,384]{3,2,1,0:T(8,128)(2,1)S(1)}, bf16[2,2,256,384]{3,2,1,0:T(8,128)(2,1)S(1)}, u32[]{:S(2)}, u32[]{:S(2)}) collective-permute-start(bf16[2,2,256,384]{3,2,1,0:T(8,128)(2,1)S(1)} %pad_maximum_fusion.rest_0_), channel_id=1, source_target_pairs={{0,4},{2,6},{4,0},{6,2},{8,12},{10,14},{12,8},{14,10},{16,20},{18,... | collective-permute-start | bytes 2359304 | tf_op jit(solution)/shard_map/ppermute | solution.py:209
  59.3 5.0 %copy-start.13 = (bf16[2,2,256,384]{3,2,1,0:T(8,128)(2,1)}, bf16[2,2,256,384]{3,2,1,0:T(8,128)(2,1)S(1)}, u32[]{:S(2)}) copy-start(bf16[2,2,256,384]{3,2,1,0:T(8,128)(2,1)S(1)} %collective-permute-done.3.x_ref) | copy-start | bytes 2359300
  59.4 1.3 copy-start.3
  60.7 1.0 copy-start.24
  60.8 3.5 %collective-permute-start.8 = (bf16[4,2,256,384]{3,2,1,0:T(8,128)(2,1)S(1)}, bf16[4,2,256,384]{3,2,1,0:T(8,128)(2,1)S(1)}, u32[]{:S(2)}, u32[]{:S(2)}) collective-permute-start(bf16[4,2,256,384]{3,2,1,0:T(8,128)(2,1)S(1)} %core_swap_1.1), channel_id=1, source_target_pairs={{0,2},{2,0},{4,6},{6,4},{8,10},{10,8},{12,14},{14,12},{16,18},{18,... | collective-permute-start | bytes 4718600 | tf_op jit(solution)/shard_map/ppermute | solution.py:209
  61.7 13.1 %collective-permute-start.9 = (bf16[4,2,128,256]{3,2,1,0:T(8,128)(2,1)S(1)}, bf16[4,2,128,256]{3,2,1,0:T(8,128)(2,1)S(1)}, u32[]{:S(2)}, u32[]{:S(2)}) collective-permute-start(bf16[4,2,128,256]{3,2,1,0:T(8,128)(2,1)S(1)} %copy-done.24), channel_id=1, source_target_pairs={{0,2},{2,0},{4,6},{6,4},{8,10},{10,8},{12,14},{14,12},{16,18},{18,... | collective-permute-start | bytes 1572872 | tf_op jit(solution)/shard_map/ppermute | solution.py:209
  64.3 1.2 copy-start.23
  65.5 9.4 %copy-start.4 = (bf16[4,2,128,256]{3,2,1,0:T(8,128)(2,1)S(1)}, bf16[4,2,128,256]{3,2,1,0:T(8,128)(2,1)}, u32[]{:S(2)}) copy-start(bf16[4,2,128,256]{3,2,1,0:T(8,128)(2,1)} %get-tuple-element.44.refs_0_.even_ref) | copy-start | bytes 1572868
  74.9 1.0 copy-start.7
  76.0 11.8 %copy-start.19 = (bf16[2,2,128,256]{3,2,1,0:T(8,128)(2,1)}, bf16[2,2,128,256]{3,2,1,0:T(8,128)(2,1)S(1)}, u32[]{:S(2)}) copy-start(bf16[2,2,128,256]{3,2,1,0:T(8,128)(2,1)S(1)} %get-tuple-element.51.rest_2_) | copy-start | bytes 786436
  76.1 21.3 %collective-permute-start.11 = (bf16[2,2,128,256]{3,2,1,0:T(8,128)(2,1)S(1)}, bf16[2,2,128,256]{3,2,1,0:T(8,128)(2,1)S(1)}, u32[]{:S(2)}, u32[]{:S(2)}) collective-permute-start(bf16[2,2,128,256]{3,2,1,0:T(8,128)(2,1)S(1)} %get-tuple-element.51.rest_2_), channel_id=1, source_target_pairs={{0,4},{2,6},{4,0},{6,2},{8,12},{10,14},{12,8},{14,10},{16,20},{18,... | collective-permute-start | bytes 786440 | tf_op jit(solution)/shard_map/ppermute | solution.py:209
  87.8 11.3 %collective-permute-start.10 = (bf16[4,2,128,256]{3,2,1,0:T(8,128)(2,1)}, bf16[4,2,128,256]{3,2,1,0:T(8,128)(2,1)S(1)}, u32[]{:S(2)}, u32[]{:S(2)}) collective-permute-start(bf16[4,2,128,256]{3,2,1,0:T(8,128)(2,1)} %get-tuple-element.54), channel_id=1, source_target_pairs={{0,2},{2,0},{4,6},{6,4},{8,10},{10,8},{12,14},{14,12},{16,18},{18,... | collective-permute-start | bytes 1572872 | tf_op jit(solution)/shard_map/ppermute | solution.py:209
  87.8 11.3 %copy-start.8 = (bf16[4,2,128,256]{3,2,1,0:T(8,128)(2,1)S(1)}, bf16[4,2,128,256]{3,2,1,0:T(8,128)(2,1)}, u32[]{:S(2)}) copy-start(bf16[4,2,128,256]{3,2,1,0:T(8,128)(2,1)} %get-tuple-element.50.refs_0_.even_ref) | copy-start | bytes 1572868
  96.9 36.3 %collective-permute-start.18 = (bf16[4,2,128,256]{3,2,1,0:T(8,128)(2,1)}, bf16[4,2,128,256]{3,2,1,0:T(8,128)(2,1)S(1)}, u32[]{:S(2)}, u32[]{:S(2)}) collective-permute-start(bf16[4,2,128,256]{3,2,1,0:T(8,128)(2,1)} %get-tuple-element.68), channel_id=1, source_target_pairs={{0,2},{2,0},{4,6},{6,4},{8,10},{10,8},{12,14},{14,12},{16,18},{18,... | collective-permute-start | bytes 1572872 | tf_op jit(solution)/shard_map/ppermute | solution.py:209
  97.4 1.0 copy-start
  99.2 1.0 copy-start.1
  101.1 9.0 %copy-start.18 = (bf16[2,2,128,256]{3,2,1,0:T(8,128)(2,1)S(1)}, bf16[2,2,128,256]{3,2,1,0:T(8,128)(2,1)}, u32[]{:S(2)}) copy-start(bf16[2,2,128,256]{3,2,1,0:T(8,128)(2,1)} %copy-done.17) | copy-start | bytes 786436
  101.1 30.2 %copy-start.21 = (bf16[2,128,256]{2,1,0:T(8,128)(2,1)S(1)}, bf16[2,128,256]{2,1,0:T(8,128)(2,1)}, u32[]{:S(2)}) copy-start(bf16[2,128,256]{2,1,0:T(8,128)(2,1)} %copy-done.20) | copy-start | bytes 393220
  101.1 32.1 %copy-start.2 = (bf16[4,2,128,256]{3,2,1,0:T(8,128)(2,1)S(1)}, bf16[4,2,128,256]{3,2,1,0:T(8,128)(2,1)}, u32[]{:S(2)}) copy-start(bf16[4,2,128,256]{3,2,1,0:T(8,128)(2,1)} %get-tuple-element.55.refs_0_.even_ref) | copy-start | bytes 1572868
  110.1 26.5 %collective-permute-start.15 = (bf16[4,2,128,256]{3,2,1,0:T(8,128)(2,1)}, bf16[4,2,128,256]{3,2,1,0:T(8,128)(2,1)S(1)}, u32[]{:S(2)}, u32[]{:S(2)}) collective-permute-start(bf16[4,2,128,256]{3,2,1,0:T(8,128)(2,1)} %get-tuple-element.64), channel_id=1, source_target_pairs={{0,2},{2,0},{4,6},{6,4},{8,10},{10,8},{12,14},{14,12},{16,18},{18,... | collective-permute-start | bytes 1572872 | tf_op jit(solution)/shard_map/ppermute | solution.py:209
  110.1 26.5 %collective-permute-start.14 = (bf16[2,2,128,256]{3,2,1,0:T(8,128)(2,1)S(1)}, bf16[2,2,128,256]{3,2,1,0:T(8,128)(2,1)S(1)}, u32[]{:S(2)}, u32[]{:S(2)}) collective-permute-start(bf16[2,2,128,256]{3,2,1,0:T(8,128)(2,1)S(1)} %copy-done.18), channel_id=1, source_target_pairs={{0,4},{2,6},{4,0},{6,2},{8,12},{10,14},{12,8},{14,10},{16,20},{18,... | collective-permute-start | bytes 786440 | tf_op jit(solution)/shard_map/ppermute | solution.py:209
  129.9 10.0 %collective-permute-start.12 = (bf16[2,128,256]{2,1,0:T(8,128)(2,1)S(1)}, bf16[2,128,256]{2,1,0:T(8,128)(2,1)S(1)}, u32[]{:S(2)}, u32[]{:S(2)}) collective-permute-start(bf16[2,128,256]{2,1,0:T(8,128)(2,1)S(1)} %get-tuple-element.62), channel_id=1, source_target_pairs={{16,0},{18,2},{20,4},{22,6},{24,8},{26,10},{28,12},{30,14},{17,1},... | collective-permute-start | bytes 393224 | tf_op jit(solution)/shard_map/ppermute | solution.py:205
  131.2 8.7 %collective-permute-start.13 = (bf16[2,128,256]{2,1,0:T(8,128)(2,1)S(1)}, bf16[2,128,256]{2,1,0:T(8,128)(2,1)S(1)}, u32[]{:S(2)}, u32[]{:S(2)}) collective-permute-start(bf16[2,128,256]{2,1,0:T(8,128)(2,1)S(1)} %copy-done.21), channel_id=1, source_target_pairs={{8,0},{10,2},{12,4},{14,6},{16,8},{18,10},{20,12},{22,14},{24,16},... | collective-permute-start | bytes 393224 | tf_op jit(solution)/shard_map/ppermute | solution.py:205
  133.2 1.0 copy-start.5
  134.2 5.8 %copy-start.6 = (bf16[4,2,128,256]{3,2,1,0:T(8,128)(2,1)S(1)}, bf16[4,2,128,256]{3,2,1,0:T(8,128)(2,1)}, u32[]{:S(2)}) copy-start(bf16[4,2,128,256]{3,2,1,0:T(8,128)(2,1)} %get-tuple-element.69.refs_0_.even_ref) | copy-start | bytes 1572868
  134.4 8.3 %collective-permute-start.19 = (bf16[2,2,128,256]{3,2,1,0:T(8,128)(2,1)S(1)}, bf16[2,2,128,256]{3,2,1,0:T(8,128)(2,1)S(1)}, u32[]{:S(2)}, u32[]{:S(2)}) collective-permute-start(bf16[2,2,128,256]{3,2,1,0:T(8,128)(2,1)S(1)} %get-tuple-element.71), channel_id=1, source_target_pairs={{0,4},{2,6},{4,0},{6,2},{8,12},{10,14},{12,8},{14,10},{16,20},{18,... | collective-permute-start | bytes 786440 | tf_op jit(solution)/shard_map/ppermute | solution.py:209
  136.7 9.3 %collective-permute-start.16 = (bf16[2,128,256]{2,1,0:T(8,128)(2,1)S(1)}, bf16[2,128,256]{2,1,0:T(8,128)(2,1)S(1)}, u32[]{:S(2)}, u32[]{:S(2)}) collective-permute-start(bf16[2,128,256]{2,1,0:T(8,128)(2,1)S(1)} %get-tuple-element.66), channel_id=1, source_target_pairs={{16,0},{18,2},{20,4},{22,6},{24,8},{26,10},{28,12},{30,14},{17,1},... | collective-permute-start | bytes 393224 | tf_op jit(solution)/shard_map/ppermute | solution.py:205
  138.0 9.7 %collective-permute-start.17 = (bf16[2,128,256]{2,1,0:T(8,128)(2,1)S(1)}, bf16[2,128,256]{2,1,0:T(8,128)(2,1)S(1)}, u32[]{:S(2)}, u32[]{:S(2)}) collective-permute-start(bf16[2,128,256]{2,1,0:T(8,128)(2,1)S(1)} %get-tuple-element.67), channel_id=1, source_target_pairs={{8,0},{10,2},{12,4},{14,6},{16,8},{18,10},{20,12},{22,14},{24,16},... | collective-permute-start | bytes 393224 | tf_op jit(solution)/shard_map/ppermute | solution.py:205
  140.1 15.8 %collective-permute-start.23 = (bf16[2,2,128,256]{3,2,1,0:T(8,128)(2,1)S(1)}, bf16[2,2,128,256]{3,2,1,0:T(8,128)(2,1)S(1)}, u32[]{:S(2)}, u32[]{:S(2)}) collective-permute-start(bf16[2,2,128,256]{3,2,1,0:T(8,128)(2,1)S(1)} %get-tuple-element.72.refs_0_), channel_id=1, source_target_pairs={{0,4},{2,6},{4,0},{6,2},{8,12},{10,14},{12,8},{14,10},{16,20},{18,... | collective-permute-start | bytes 786440 | tf_op jit(solution)/shard_map/ppermute | solution.py:209
  142.8 8.7 %collective-permute-start.20 = (bf16[2,128,256]{2,1,0:T(8,128)(2,1)S(1)}, bf16[2,128,256]{2,1,0:T(8,128)(2,1)S(1)}, u32[]{:S(2)}, u32[]{:S(2)}) collective-permute-start(bf16[2,128,256]{2,1,0:T(8,128)(2,1)S(1)} %get-tuple-element.74), channel_id=1, source_target_pairs={{16,0},{18,2},{20,4},{22,6},{24,8},{26,10},{28,12},{30,14},{17,1},... | collective-permute-start | bytes 393224 | tf_op jit(solution)/shard_map/ppermute | solution.py:205
  144.1 10.1 %collective-permute-start.21 = (bf16[2,128,256]{2,1,0:T(8,128)(2,1)S(1)}, bf16[2,128,256]{2,1,0:T(8,128)(2,1)S(1)}, u32[]{:S(2)}, u32[]{:S(2)}) collective-permute-start(bf16[2,128,256]{2,1,0:T(8,128)(2,1)S(1)} %get-tuple-element.75), channel_id=1, source_target_pairs={{8,0},{10,2},{12,4},{14,6},{16,8},{18,10},{20,12},{22,14},{24,16},... | collective-permute-start | bytes 393224 | tf_op jit(solution)/shard_map/ppermute | solution.py:205
  154.4 7.4 %collective-permute-start.22 = (bf16[3,2,128,128]{2,3,1,0:T(8,128)(2,1)S(1)}, bf16[3,2,128,128]{2,3,1,0:T(8,128)(2,1)S(1)}, u32[]{:S(2)}, u32[]{:S(2)}) collective-permute-start(bf16[3,2,128,128]{2,3,1,0:T(8,128)(2,1)S(1)} %constant_dynamic-slice_fusion), channel_id=1, source_target_pairs={{0,1},{1,0},{2,3},{3,2},{4,5},{5,4},{6,7},{7,6},{8,9},{9,8},{10,11... | collective-permute-start | bytes 589832 | tf_op jit(solution)/shard_map/ppermute | solution.py:218
  156.0 5.9 %collective-permute-start.24 = (bf16[2,128,256]{2,1,0:T(8,128)(2,1)S(1)}, bf16[2,128,256]{2,1,0:T(8,128)(2,1)S(1)}, u32[]{:S(2)}, u32[]{:S(2)}) collective-permute-start(bf16[2,128,256]{2,1,0:T(8,128)(2,1)S(1)} %get-tuple-element.78), channel_id=1, source_target_pairs={{16,0},{18,2},{20,4},{22,6},{24,8},{26,10},{28,12},{30,14},{17,1},... | collective-permute-start | bytes 393224 | tf_op jit(solution)/shard_map/ppermute | solution.py:205
  158.6 9.2 %collective-permute-start.25 = (bf16[2,128,256]{2,1,0:T(8,128)(2,1)S(1)}, bf16[2,128,256]{2,1,0:T(8,128)(2,1)S(1)}, u32[]{:S(2)}, u32[]{:S(2)}) collective-permute-start(bf16[2,128,256]{2,1,0:T(8,128)(2,1)S(1)} %get-tuple-element.79), channel_id=1, source_target_pairs={{8,0},{10,2},{12,4},{14,6},{16,8},{18,10},{20,12},{22,14},{24,16},... | collective-permute-start | bytes 393224 | tf_op jit(solution)/shard_map/ppermute | solution.py:205
  167.9 4.3 %collective-permute-start.26 = (bf16[2,128,128]{1,2,0:T(8,128)(2,1)S(1)}, bf16[2,128,128]{1,2,0:T(8,128)(2,1)S(1)}, u32[]{:S(2)}, u32[]{:S(2)}) collective-permute-start(bf16[2,128,128]{1,2,0:T(8,128)(2,1)S(1)} %dynamic-slice_bitcast_fusion), channel_id=1, source_target_pairs={{0,1},{1,0},{2,3},{3,2},{4,5},{5,4},{6,7},{7,6},{8,9},{9,8},{10,11... | collective-permute-start | bytes 196616 | tf_op jit(solution)/shard_map/ppermute | solution.py:218
  (5 other events, 4.1 us)
where the time goes:
time: 177 us; the launch traced here: 174 us
  starting transfers between devices  68.3 us (39%)
  waiting for transfers between devices  53 us (30%)
  Pallas kernels  37.4 us (21%)
  local copies, waits for them, and re-layouts  13.4 us (8%)
    pallas_call x4, Pallas kernels, attend_group(): pl.pallas_call(functools.partial(group_kernel, heads, unread), grid_spec=...  36.3 us
    ppermute x12, starting transfers between devices, swapped(): lax.ppermute(value, 'ctx', [(place, place ^ bit) for place in range(lax.a...  36.1 us
    ppermute x12, starting transfers between devices, shifted(): lax.ppermute(value, 'ctx', [(source, source + steps) for source in sources])  28.5 us
    ppermute x12, waiting for transfers between devices, shifted(): lax.ppermute(value, 'ctx', [(source, source + steps) for source in sources])  23 us
    ppermute x12, waiting for transfers between devices, swapped(): lax.ppermute(value, 'ctx', [(place, place ^ bit) for place in range(lax.a...  19.8 us
    unnamed x61, local copies, waits for them, and re-layouts  13.4 us
    ppermute x3, waiting for transfers between devices, tp_received(): lax.ppermute(sent, 'tp', [(place, (place + step) % count) for place in ra...  10.3 us
    ppermute x3, starting transfers between devices, tp_received(): lax.ppermute(sent, 'tp', [(place, (place + step) % count) for place in ra...  3.74 us
  transfers between devices with their start and end apart: 27, of which 14 were waited for; matrix products, arithmetic and copies ran while one was open for 0% of the time, Pallas kernels for 21%

commit v1 on v0

--- a/solution.py
+++ b/solution.py
@@ -20,13 +20,26 @@
     return jnp.dot(a, b, preferred_element_type=jnp.float32)
 
 
-def group_kernel(heads, unread, own, doc_lengths, q_ref, g_ref, own_ref, far_ref, x_ref, c_ref, *rest):
-    out_ref, dq_ref, even_ref, odd_ref, *scratch = rest[unread:]
+def dot_rows(a, b):
+    return lax.dot_general(a, b, (((1,), (1,)), ((), ())), preferred_element_type=jnp.float32)
+
+
+def group_kernel(
+    group, heads, unread, own, doc_lengths,
+    q_ref, g_hbm, q_turned, g_turned_hbm, own_ref, far_ref, x_ref, c_ref, *rest,
+):
+    out_hbm, dq_ref, even_ref, odd_ref, *scratch = rest[unread:]
     (
-        q_all, q_turned, g_all, g_turned, k_win, v_win, k_turned, v_turned,
-        bias, scores, weights, grads, highest, summed, delta, dq_acc,
+        q_all, g_all, k_win, v_win, g_ref, g_turned, out_ref,
+        bias, scores, weights, grads, highest, summed, delta, dq_acc, arrivals,
     ) = scratch
-    rows = q_ref.shape[0]
+    rows, width = q_ref.shape
+    own_columns = pl.ds(group * width, width)
+    g_copy = pltpu.make_async_copy(g_hbm.at[:, own_columns], g_ref, arrivals.at[0])
+    g_turned_copy = pltpu.make_async_copy(g_turned_hbm.at[group], g_turned, arrivals.at[1])
+    out_copy = pltpu.make_async_copy(out_ref, out_hbm.at[:, own_columns], arrivals.at[2])
+    g_copy.start()
+    g_turned_copy.start()
     at_once = min(heads, HEADS_AT_ONCE)
     repeats = 2 * rows // HEAD_SIZE
     first = own[0] * rows
@@ -43,7 +56,6 @@
 
     for span, column in zip(spans, columns):
         q_all[span, :] = q_ref[:, column]
-        q_turned[:, span] = q_ref[:, column].T
     window_refs = [
         own_ref, c_ref.at[0], x_ref.at[0], c_ref.at[1], far_ref, c_ref.at[2], x_ref.at[1], c_ref.at[3]
     ]
@@ -52,8 +64,6 @@
         k_win[pair, here, :] = source[0]
         v_win[pair, here, :HEAD_SIZE] = source[1]
         v_win[pair, here, HEAD_SIZE:] = jnp.ones((rows, HEAD_SIZE), jnp.bfloat16)
-        k_turned[pair, :, here] = source[0].T
-        v_turned[pair, :, here] = source[1].T
     query_pos = first + lax.broadcasted_iota(jnp.int32, (rows, HEAD_SIZE), 0)
     low = jnp.zeros((rows, HEAD_SIZE), jnp.int32)
     start = 0
@@ -74,7 +84,7 @@
             allowed = (key_pos >= low) & (key_pos <= query_pos)
             bias[:, place * HEAD_SIZE : (place + 1) * HEAD_SIZE] = jnp.where(allowed, 0.0, MASKED)
         for batch in batches:
-            part = dot(q_all[batch, :], k_turned[pair])
+            part = dot_rows(q_all[batch, :], k_win[pair])
             for head in range(at_once):
                 here = slice(batch.start + head * rows, batch.start + (head + 1) * rows)
                 piece = part[head * rows : (head + 1) * rows] * (SCORE_SCALE * LOG2E) + bias[...]
@@ -99,22 +109,31 @@
         return carry
 
     lax.fori_loop(0, trips, sum_pair, 0)
-    ones = jnp.ones((2 * HEAD_SIZE, HEAD_SIZE), jnp.bfloat16)
-    for span, column in zip(spans, columns):
+    g_copy.wait()
+    g_turned_copy.wait()
+    lane = lax.broadcasted_iota(jnp.int32, (rows, HEAD_SIZE), 1)
+    inverses = jnp.zeros((rows, HEAD_SIZE), jnp.float32)
+    for head, (span, column) in enumerate(zip(spans, columns)):
         inverse = 1.0 / summed[span, HEAD_SIZE:]
+        inverses = jnp.where(lane == head, inverse, inverses)
         output = (summed[span, :HEAD_SIZE] * inverse).astype(jnp.bfloat16)
         out_ref[:, column] = output
         scaled = (g_ref[:, column].astype(jnp.float32) * inverse).astype(jnp.bfloat16)
         g_all[span, :] = scaled
-        g_turned[:, span] = scaled.T
         terms = output.astype(jnp.float32) * scaled.astype(jnp.float32)
         upper = terms.astype(jnp.bfloat16)
-        lower = (terms - upper.astype(jnp.float32)).astype(jnp.bfloat16)
-        delta[span, :] = dot(jnp.concatenate([upper, lower], axis=1), ones)
+        grads[span, :HEAD_SIZE] = upper
+        grads[span, HEAD_SIZE : 2 * HEAD_SIZE] = (terms - upper.astype(jnp.float32)).astype(jnp.bfloat16)
+    out_copy.start()
+    delta[...] = dot(grads[:, : 2 * HEAD_SIZE], jnp.ones((2 * HEAD_SIZE, HEAD_SIZE), jnp.bfloat16))
+    inverses = inverses.T
+    for head, span in enumerate(spans):
+        turned = g_turned[:, span].astype(jnp.float32) * inverses[head : head + 1, :]
+        g_turned[:, span] = turned.astype(jnp.bfloat16)
 
     def grad_pair(pair, carry):
         for batch in batches:
-            part = dot(g_all[batch, :], v_turned[pair])
+            part = dot_rows(g_all[batch, :], v_win[pair, :, :HEAD_SIZE])
             for head in range(at_once):
                 here = slice(batch.start + head * rows, batch.start + (head + 1) * rows)
                 piece = part[head * rows : (head + 1) * rows] - jnp.concatenate([delta[here, :]] * repeats, axis=1)
@@ -138,9 +157,33 @@
 
     for span, column in zip(spans, columns):
         dq_ref[:, column] = (dq_acc[span, :] * SCORE_SCALE).astype(jnp.bfloat16)
-
-
-def attend_group(group, groups, own, doc_lengths, queries, gradient, window, place, buffers, before):
+    out_copy.wait()
+
+
+def turn_kernel(heads, ref, out):
+    rows = ref.shape[0]
+    for head in range(heads):
+        out[0, :, head * rows : (head + 1) * rows] = ref[:, head * HEAD_SIZE : (head + 1) * HEAD_SIZE].T
+
+
+def turned_heads(values, groups, name):
+    rows, width = values.shape
+    columns = width // groups
+    heads = columns // HEAD_SIZE
+    return pl.pallas_call(
+        functools.partial(turn_kernel, heads),
+        grid=(groups,),
+        in_specs=[pl.BlockSpec((rows, columns), lambda i: (0, i))],
+        out_specs=pl.BlockSpec((1, HEAD_SIZE, heads * rows), lambda i: (i, 0, 0)),
+        out_shape=jax.ShapeDtypeStruct((groups, HEAD_SIZE, heads * rows), jnp.bfloat16),
+        cost_estimate=pl.CostEstimate(flops=0, bytes_accessed=8 * values.size, transcendentals=0),
+        name=name,
+    )(values)
+
+
+def attend_group(
+    group, groups, own, doc_lengths, queries, gradient, turned_q, turned_g, window, place, buffers, before
+):
     rows, width = queries.shape
     columns = width // groups
     heads = columns // HEAD_SIZE
@@ -156,22 +199,27 @@
     short = lambda *shape: pltpu.VMEM(shape, jnp.bfloat16)
     full = lambda *shape: pltpu.VMEM(shape, jnp.float32)
     return pl.pallas_call(
-        functools.partial(group_kernel, heads, unread),
+        functools.partial(group_kernel, group, heads, unread),
         grid_spec=pltpu.PrefetchScalarGridSpec(
             num_scalar_prefetch=2,
             grid=(1,),
-            in_specs=[block, block, shard, shard, several(half // 2), several(half)]
+            in_specs=[
+                block,
+                pl.BlockSpec(memory_space=pl.ANY),
+                pl.BlockSpec((None, HEAD_SIZE, stacked), lambda i, *_: (group, 0, 0)),
+                pl.BlockSpec(memory_space=pl.ANY),
+                shard, shard, several(half // 2), several(half),
+            ]
             + [pl.BlockSpec(memory_space=pl.ANY)] * unread,
-            out_specs=[block, block, grads_block, grads_block],
+            out_specs=[pl.BlockSpec(memory_space=pl.ANY), block, grads_block, grads_block],
             scratch_shapes=[
                 short(stacked, HEAD_SIZE),
-                short(HEAD_SIZE, stacked),
                 short(stacked, HEAD_SIZE),
-                short(HEAD_SIZE, stacked),
                 short(half, 2 * rows, HEAD_SIZE),
                 short(half, 2 * rows, 2 * HEAD_SIZE),
-                short(half, HEAD_SIZE, 2 * rows),
-                short(half, HEAD_SIZE, 2 * rows),
+                short(rows, columns),
+                short(HEAD_SIZE, stacked),
+                short(rows, columns),
                 full(rows, 2 * rows),
                 full(half, stacked, 2 * rows),
                 short(half, stacked, 2 * rows),
@@ -180,6 +228,7 @@
                 full(stacked, 2 * HEAD_SIZE),
                 full(stacked, HEAD_SIZE),
                 full(stacked, HEAD_SIZE),
+                pltpu.SemaphoreType.DMA((3,)),
             ],
         ),
         out_shape=[
@@ -188,7 +237,7 @@
             grads,
             grads,
         ],
-        input_output_aliases={8 + number: number for number in range(len(buffers))},
+        input_output_aliases={10 + number: number for number in range(len(buffers))},
         compiler_params=pltpu.CompilerParams(vmem_limit_bytes=56 * 1024 * 1024),
         cost_estimate=pl.CostEstimate(
             flops=4 * 6 * 2 * heads * rows * keys * HEAD_SIZE,
@@ -196,7 +245,7 @@
             transcendentals=heads * rows * keys,
         ),
         name=f"attend_group_{group}",
-    )(own, doc_lengths, queries, gradient, *window, *buffers, *before)
+    )(own, doc_lengths, queries, gradient, turned_q, turned_g, *window, *buffers, *before)
 
 
 def shifted(value, steps):
@@ -236,19 +285,25 @@
     return pl.BlockSpec(shape, lambda i, *_: (0,) * len(shape))
 
 
-def small_kernel(kernel, scalars, operands, specs, outs, before, name):
+def small_kernel(kernel, scalars, operands, specs, outs, before, name, through=()):
+    if through:
+        inner, handed = kernel, len(through)
+        kernel = lambda *refs: inner(*refs[:-handed])
+    first = 1 + len(operands) + len(before)
     return pl.pallas_call(
         kernel,
         grid_spec=pltpu.PrefetchScalarGridSpec(
             num_scalar_prefetch=1,
             grid=(1,),
-            in_specs=specs + [pl.BlockSpec(memory_space=pl.ANY)] * len(before),
-            out_specs=[whole_block(shape) for shape in outs],
+            in_specs=specs + [pl.BlockSpec(memory_space=pl.ANY)] * (len(before) + len(through)),
+            out_specs=[whole_block(shape) for shape in outs] + [pl.BlockSpec(memory_space=pl.ANY)] * len(through),
         ),
-        out_shape=[jax.ShapeDtypeStruct(shape, jnp.bfloat16) for shape in outs],
+        out_shape=[jax.ShapeDtypeStruct(shape, jnp.bfloat16) for shape in outs]
+        + [jax.ShapeDtypeStruct(part.shape, part.dtype) for part in through],
+        input_output_aliases={first + number: len(outs) + number for number in range(len(through))},
         compiler_params=pltpu.CompilerParams(vmem_limit_bytes=32 * 1024 * 1024),
         name=name,
-    )(scalars, *operands, *before)
+    )(scalars, *operands, *before, *through)
 
 
 def pack_for_tp(key_vectors, value_vectors, groups, tp_own):
@@ -358,7 +413,7 @@
     )
 
 
-def fold_x(sent, kept, own, before, name):
+def fold_x(sent, kept, own, before, name, through=()):
     got = swapped(sent, 2)
 
     def kernel(own, kept_ref, got_ref, *refs):
@@ -374,8 +429,26 @@
                     out[...] = total.astype(out.dtype)
 
     return small_kernel(
-        kernel, own, [kept, got], [whole_block(kept.shape), whole_block(got.shape)], [kept.shape[1:]] * 3, before, name
+        kernel, own, [kept, got], [whole_block(kept.shape), whole_block(got.shape)], [kept.shape[1:]] * 3, before, name, through,
     )
+
+
+def finish(parts, own, before, name):
+    count = len(parts)
+    operands = [array for part in parts for array in part]
+    kinds, depth, rows = operands[0].shape
+
+    def kernel(own, *refs):
+        out = refs[-1]
+        for index in range(count):
+            near, far, beyond = refs[3 * index : 3 * index + 3]
+            for kind in range(kinds):
+                out[index, kind] = (wide(near[kind]) + wide(far[kind]) + wide(beyond[kind])).T.astype(out.dtype)
+
+    return small_kernel(
+        kernel, own, operands, [whole_block(part.shape) for part in operands],
+        [(count, kinds, rows, depth)], before, name,
+    )[0]
 
 
 def body(queries, key_vectors, value_vectors, output_gradient, doc_lengths):
@@ -393,33 +466,40 @@
     received = tp_received(lambda place, step: packed[step - 1])
     chunks = join_tokens(key_vectors, value_vectors, received, groups, bounds, tp_info)
     evens = [even_window(chunk, own) for chunk in chunks]
+    turned_q = turned_heads(queries, groups, "turn_queries")
+    turned_g = turned_heads(output_gradient, groups, "turn_gradient")
 
     windows = [whole_window(evens[0], own_info, [], "core_swap_0")]
     buffers = ()
-    results, got, folded, sums = [], [], [], []
+    results, got, folded, sums, parts = [], [], [], [], []
 
     def fold_next_cores(before):
         group = len(folded)
         folded.append(fold_cores(results[group][2], got[group], own_info, before, f"fold_cores_{group}"))
 
-    def fold_next_x(before):
+    def fold_next_x(before, through=()):
         group = len(sums)
-        sums.append(fold_x(*folded[group], own_info, before, f"fold_x_{group}"))
+        near, far, beyond, *handed = fold_x(*folded[group], own_info, before, f"fold_x_{group}", through)
+        sums.append(near)
+        parts.append((near, shifted(far, -(WINDOW // 2)), shifted(beyond, -WINDOW)))
+        return handed
 
     for group in range(groups):
         waits = [evens[1][3]] if group == 0 and groups > 1 else []
         if group >= 2:
             waits.append(folded[group - 2][0])
         if group >= 3:
-            waits.append(sums[group - 3][1])
+            waits.append(sums[group - 3])
         chunk = min(group, 1)
         results.append(
             attend_group(
-                group, groups, own_info, doc_lengths, queries, output_gradient, windows[chunk], group - chunk,
-                buffers, waits,
+                group, groups, own_info, doc_lengths, queries, output_gradient, turned_q, turned_g,
+                windows[chunk], group - chunk, buffers, waits,
             )
         )
         *buffers, even, odd = results[-1]
+        if 3 <= groups == group + 1:
+            (odd,) = fold_next_x([array for part in parts for array in part[1:]], [odd])
         got.append(swapped(odd, 1))
         if group == 0 and groups > 1:
             windows.append(whole_window(evens[1], own_info, [even], "core_swap_1"))
@@ -427,17 +507,10 @@
             fold_next_cores([even])
         if group >= 2 and group < groups - 1:
             fold_next_x([even])
-    while len(sums) < groups - 2:
-        fold_next_x([got[-1]])
     fold_next_cores([])
     while len(sums) < groups:
         fold_next_x([folded[-1][0]] if len(sums) < groups - 1 else [])
 
-    totals = []
-    for near, far, beyond in sums:
-        total = wide(near) + wide(shifted(beyond, -WINDOW)) + wide(shifted(far, -(WINDOW // 2)))
-        totals.append(jnp.swapaxes(total.astype(jnp.bfloat16), 1, 2))
-
     def exchanged(total):
         def tokens_of(place, step=0):
             return lax.dynamic_slice_in_dim(total, place * local, local, total.ndim - 2)
@@ -445,11 +518,11 @@
         return in_tp_order(tokens_of(tp_own), tp_received(tokens_of))
 
     if groups > 1:
-        early = exchanged(jnp.stack(totals[:-1]))
-        late = exchanged(totals[-1])
-        ordered = [[*(part[group] for group in range(groups - 1)), last] for part, last in zip(early, late)]
+        early = exchanged(finish(parts[:-1], own_info, [sums[-1]], "finish_early"))
+        late = exchanged(finish(parts[-1:], own_info, [], "finish_late"))
+        ordered = [[*(part[group] for group in range(groups - 1)), last[0]] for part, last in zip(early, late)]
     else:
-        ordered = [[part] for part in exchanged(totals[0])]
+        ordered = [[part[0]] for part in exchanged(finish(parts, own_info, [], "finish_late"))]
 
     def output(which):
         return jnp.concatenate([part[which] for source in ordered for part in source], axis=1)

time: 177 us -> 181 us (1.023)
  the two profiles are of different devices: /device:TPU:18 before, /device:TPU:0 now
where the time goes in v1:
time: 181 us; the launch traced here: 180 us
  waiting for transfers between devices  73.4 us (41%)
  starting transfers between devices  48.6 us (27%)
  Pallas kernels  44.7 us (25%)
  local copies, waits for them, and re-layouts  11.2 us (6%)
    ppermute x12, waiting for transfers between devices, shifted(): lax.ppermute(value, 'ctx', [(source, source + steps) for source in sources])  41.9 us
    pallas_call x4, Pallas kernels, attend_group(): pl.pallas_call(functools.partial(group_kernel, group, heads, unread), gri...  35 us
    ppermute x12, starting transfers between devices, shifted(): lax.ppermute(value, 'ctx', [(source, source + steps) for source in sources])  25.4 us
    ppermute x12, waiting for transfers between devices, swapped(): lax.ppermute(value, 'ctx', [(place, place ^ bit) for place in range(lax.a...  22.7 us
    ppermute x12, starting transfers between devices, swapped(): lax.ppermute(value, 'ctx', [(place, place ^ bit) for place in range(lax.a...  17 us
    unnamed x59, local copies, waits for them, and re-layouts  11.2 us
    ppermute x3, waiting for transfers between devices, tp_received(): lax.ppermute(sent, 'tp', [(place, (place + step) % count) for place in ra...  8.87 us
    pallas_call x2, Pallas kernels, turned_heads(): pl.pallas_call(functools.partial(turn_kernel, heads), grid=(groups,), in_...  8.27 us
  transfers between devices with their start and end apart: 27, of which 14 were waited for; matrix products, arithmetic and copies ran while one was open for 0% of the time, Pallas kernels for 25%

profile of v1, /device:TPU:0, one launch (start us, length us, event | category | flops | bytes accessed | tf_op | source)
XLA Modules:
  0.0 179.6 jit_solution(3144329569092679127)
XLA Ops:
  0.6 0.9 copy-done.10
  1.6 0.9 copy-done.11
  2.6 3.0 %collective-permute-start = (bf16[2,128,512]{2,1,0:T(8,128)(2,1)S(1)}, bf16[2,128,512]{2,1,0:T(8,128)(2,1)S(1)}, u32[]{:S(2)}, u32[]{:S(2)}) collective-permute-start(bf16[2,128,512]{2,1,0:T(8,128)(2,1)S(1)} %pack_for_tp.1), channel_id=1, source_target_pairs={{0,1},{1,0},{2,3},{3,2},{4,5},{5,4},{6,7},{7,6},{8,9},{9,8},{10,11... | collective-permute-start | bytes 786440 | tf_op jit(solution)/shard_map/ppermute | solution.py:267
  5.6 6.3 %collective-permute-done.refs_0_ = bf16[2,128,512]{2,1,0:T(8,128)(2,1)S(1)} collective-permute-done((bf16[2,128,512]{2,1,0:T(8,128)(2,1)S(1)}, bf16[2,128,512]{2,1,0:T(8,128)(2,1)S(1)}, u32[]{:S(2)}, u32[]{:S(2)}) %collective-permute-start) | collective-permute-done | bytes 262176 | tf_op jit(solution)/shard_map/ppermute | solution.py:267
  12.0 3.7 %collective-permute-start.4 = (bf16[2,256,128]{2,1,0:T(8,128)(2,1)S(1)}, bf16[2,256,128]{2,1,0:T(8,128)(2,1)S(1)}, u32[]{:S(2)}, u32[]{:S(2)}) collective-permute-start(bf16[2,256,128]{2,1,0:T(8,128)(2,1)S(1)} %get-tuple-element.44.own_ref), channel_id=1, source_target_pairs={{0,8},{2,10},{4,12},{6,14},{8,16},{10,18},{12,20},{14,22},{16,24},... | collective-permute-start | bytes 393224 | tf_op jit(solution)/shard_map/ppermute | solution.py:254
  15.7 3.5 %collective-permute-start.1 = (bf16[2,256,384]{2,1,0:T(8,128)(2,1)S(1)}, bf16[2,256,384]{2,1,0:T(8,128)(2,1)S(1)}, u32[]{:S(2)}, u32[]{:S(2)}) collective-permute-start(bf16[2,256,384]{2,1,0:T(8,128)(2,1)S(1)} %get-tuple-element.43.own_ref), channel_id=1, source_target_pairs={{0,8},{2,10},{4,12},{6,14},{8,16},{10,18},{12,20},{14,22},{16,24},... | collective-permute-start | bytes 1179656 | tf_op jit(solution)/shard_map/ppermute | solution.py:254
  19.2 3.5 %collective-permute-start.5 = (bf16[2,256,128]{2,1,0:T(8,128)(2,1)S(1)}, bf16[2,256,128]{2,1,0:T(8,128)(2,1)S(1)}, u32[]{:S(2)}, u32[]{:S(2)}) collective-permute-start(bf16[2,256,128]{2,1,0:T(8,128)(2,1)S(1)} %collective-permute-done.4.far_ref), channel_id=1, source_target_pairs={{0,8},{2,10},{4,12},{6,14},{8,16},{10,18},{12,20},{14,22},{16,24},... | collective-permute-start | bytes 393224 | tf_op jit(solution)/shard_map/ppermute | solution.py:254
  22.8 6.6 %collective-permute-done.5.beyond_ref = bf16[2,256,128]{2,1,0:T(8,128)(2,1)S(1)} collective-permute-done((bf16[2,256,128]{2,1,0:T(8,128)(2,1)S(1)}, bf16[2,256,128]{2,1,0:T(8,128)(2,1)S(1)}, u32[]{:S(2)}, u32[]{:S(2)}) %collective-permute-start.5) | collective-permute-done | bytes 131104 | tf_op jit(solution)/shard_map/ppermute | solution.py:254
  29.5 4.4 %collective-permute-start.2 = (bf16[2,256,384]{2,1,0:T(8,128)(2,1)S(1)}, bf16[2,256,384]{2,1,0:T(8,128)(2,1)S(1)}, u32[]{:S(2)}, u32[]{:S(2)}) collective-permute-start(bf16[2,256,384]{2,1,0:T(8,128)(2,1)S(1)} %collective-permute-done.1.far_ref), channel_id=1, source_target_pairs={{0,8},{2,10},{4,12},{6,14},{8,16},{10,18},{12,20},{14,22},{16,24},... | collective-permute-start | bytes 1179656 | tf_op jit(solution)/shard_map/ppermute | solution.py:254
  33.9 1.6 collective-permute-start.6
  35.5 4.9 %collective-permute-done.6.x_ref = bf16[2,2,256,128]{3,2,1,0:T(8,128)(2,1)S(1)} collective-permute-done((bf16[2,2,256,128]{3,2,1,0:T(8,128)(2,1)S(1)}, bf16[2,2,256,128]{3,2,1,0:T(8,128)(2,1)S(1)}, u32[]{:S(2)}, u32[]{:S(2)}) %collective-permute-start.6) | collective-permute-done | bytes 262176 | tf_op jit(solution)/shard_map/ppermute | solution.py:258
  40.5 4.1 %turn_queries.1.q_turned = bf16[4,128,2048]{2,1,0:T(8,128)(2,1)} custom-call(bf16[256,4096]{1,0:T(8,128)(2,1)} %q_ref.7), custom_call_target="tpu_custom_call" | custom-call | bytes 8388608 | tf_op jit(solution)/shard_map/turn_queries/pallas_call | solution.py:173
  44.6 4.1 %turn_gradient.1.g_turned_hbm = bf16[4,128,2048]{2,1,0:T(8,128)(2,1)} custom-call(bf16[256,4096]{1,0:T(8,128)(2,1)} %g_hbm.7), custom_call_target="tpu_custom_call" | custom-call | bytes 8388608 | tf_op jit(solution)/shard_map/turn_gradient/pallas_call | solution.py:173
  48.9 1.6 collective-permute-start.3
  51.3 8.6 %attend_group_0.1 = (bf16[256,4096]{1,0:T(8,128)(2,1)}, bf16[256,4096]{1,0:T(8,128)(2,1)}, bf16[4,2,128,256]{3,2,1,0:T(8,128)(2,1)}, bf16[4,2,128,256]{3,2,1,0:T(8,128)(2,1)}) custom-call(s32[1]{0:T(128)} %bitcast.own.refs_0_, s32[8]{0:T(128)} %doc_lengths.7, bf16[256,4096]{1,0:T(8,128)(2,1)} %q_ref.7, bf16[256,4096]{1,0:T(8,128)(2,1)} %g_hbm.7, ...), custom_call_target="tpu_custom_call" | custom-call | flops 25769803776 | bytes 4194304 | tf_op jit(solution)/shard_map/attend_group_0/pallas_call | solution.py:201
  59.9 9.0 %collective-permute-done.3.x_ref = bf16[2,2,256,384]{3,2,1,0:T(8,128)(2,1)S(1)} collective-permute-done((bf16[2,2,256,384]{3,2,1,0:T(8,128)(2,1)S(1)}, bf16[2,2,256,384]{3,2,1,0:T(8,128)(2,1)S(1)}, u32[]{:S(2)}, u32[]{:S(2)}) %collective-permute-start.3) | collective-permute-done | bytes 786464 | tf_op jit(solution)/shard_map/ppermute | solution.py:258
  69.0 1.3 copy-done.3
  71.3 2.6 %collective-permute-done.8.c_ref = bf16[4,2,256,384]{3,2,1,0:T(8,128)(2,1)S(1)} collective-permute-done((bf16[4,2,256,384]{3,2,1,0:T(8,128)(2,1)S(1)}, bf16[4,2,256,384]{3,2,1,0:T(8,128)(2,1)S(1)}, u32[]{:S(2)}, u32[]{:S(2)}) %collective-permute-start.8) | collective-permute-done | bytes 1572896 | tf_op jit(solution)/shard_map/ppermute | solution.py:258
  73.9 1.2 copy-done.23
  75.1 8.9 %attend_group_1.1 = (bf16[256,4096]{1,0:T(8,128)(2,1)}, bf16[256,4096]{1,0:T(8,128)(2,1)}, bf16[4,2,128,256]{3,2,1,0:T(8,128)(2,1)}, bf16[4,2,128,256]{3,2,1,0:T(8,128)(2,1)}) custom-call(s32[1]{0:T(128)} %bitcast.own.refs_0_, s32[8]{0:T(128)} %doc_lengths.7, bf16[256,4096]{1,0:T(8,128)(2,1)} %q_ref.7, ...), custom_call_target="tpu_custom_call", output_to_operand_aliasing={{0}: (10, {}), {1}: (11, {})} | custom-call | flops 25769803776 | bytes 4194304 | tf_op jit(solution)/shard_map/attend_group_1/pallas_call | solution.py:201
  84.0 1.0 copy-done.5
  85.2 4.8 %collective-permute-start.11 = (bf16[2,2,128,256]{3,2,1,0:T(8,128)(2,1)S(1)}, bf16[2,2,128,256]{3,2,1,0:T(8,128)(2,1)S(1)}, u32[]{:S(2)}, u32[]{:S(2)}) collective-permute-start(bf16[2,2,128,256]{3,2,1,0:T(8,128)(2,1)S(1)} %get-tuple-element.52.rest_2_), channel_id=1, source_target_pairs={{0,4},{2,6},{4,0},{6,2},{8,12},{10,14},{12,8},{14,10},{16,20},{18,... | collective-permute-start | bytes 786440 | tf_op jit(solution)/shard_map/ppermute | solution.py:258
  90.0 8.8 %attend_group_2.1 = (bf16[256,4096]{1,0:T(8,128)(2,1)}, bf16[256,4096]{1,0:T(8,128)(2,1)}, bf16[4,2,128,256]{3,2,1,0:T(8,128)(2,1)}, bf16[4,2,128,256]{3,2,1,0:T(8,128)(2,1)}) custom-call(s32[1]{0:T(128)} %bitcast.own.refs_0_, s32[8]{0:T(128)} %doc_lengths.7, bf16[256,4096]{1,0:T(8,128)(2,1)} %q_ref.7, ...), custom_call_target="tpu_custom_call", output_to_operand_aliasing={{0}: (10, {}), {1}: (11, {})} | custom-call | flops 25769803776 | bytes 4194304 | tf_op jit(solution)/shard_map/attend_group_2/pallas_call | solution.py:201
  99.4 1.0 copy-done
  100.5 1.3 collective-permute-start.12
  101.8 1.3 collective-permute-start.13
  103.2 1.0 copy-done.1
  104.4 3.5 %collective-permute-start.14 = (bf16[2,2,128,256]{3,2,1,0:T(8,128)(2,1)S(1)}, bf16[2,2,128,256]{3,2,1,0:T(8,128)(2,1)S(1)}, u32[]{:S(2)}, u32[]{:S(2)}) collective-permute-start(bf16[2,2,128,256]{3,2,1,0:T(8,128)(2,1)S(1)} %get-tuple-element.57.rest_2_), channel_id=1, source_target_pairs={{0,4},{2,6},{4,0},{6,2},{8,12},{10,14},{12,8},{14,10},{16,20},{18,... | collective-permute-start | bytes 786440 | tf_op jit(solution)/shard_map/ppermute | solution.py:258
  107.9 8.7 %attend_group_3.1 = (bf16[256,4096]{1,0:T(8,128)(2,1)}, bf16[256,4096]{1,0:T(8,128)(2,1)}, bf16[4,2,128,256]{3,2,1,0:T(8,128)(2,1)}, bf16[4,2,128,256]{3,2,1,0:T(8,128)(2,1)}) custom-call(s32[1]{0:T(128)} %bitcast.own.refs_0_, s32[8]{0:T(128)} %doc_lengths.7, bf16[256,4096]{1,0:T(8,128)(2,1)} %q_ref.7, ...), custom_call_target="tpu_custom_call", output_to_operand_aliasing={{0}: (10, {}), {1}: (11, {})} | custom-call | flops 25769803776 | bytes 4194304 | tf_op jit(solution)/shard_map/attend_group_3/pallas_call | solution.py:201
  116.6 4.3 %collective-permute-done.12.refs_3_.refs_1_ = bf16[2,128,256]{2,1,0:T(8,128)(2,1)S(1)} collective-permute-done((bf16[2,128,256]{2,1,0:T(8,128)(2,1)S(1)}, bf16[2,128,256]{2,1,0:T(8,128)(2,1)S(1)}, u32[]{:S(2)}, u32[]{:S(2)}) %collective-permute-start.12) | collective-permute-done | bytes 131104 | tf_op jit(solution)/shard_map/ppermute | solution.py:254
  120.9 6.8 %collective-permute-done.13.refs_4_.refs_2_ = bf16[2,128,256]{2,1,0:T(8,128)(2,1)S(1)} collective-permute-done((bf16[2,128,256]{2,1,0:T(8,128)(2,1)S(1)}, bf16[2,128,256]{2,1,0:T(8,128)(2,1)S(1)}, u32[]{:S(2)}, u32[]{:S(2)}) %collective-permute-start.13) | collective-permute-done | bytes 131104 | tf_op jit(solution)/shard_map/ppermute | solution.py:254
  127.9 1.0 copy-done.7
  129.1 3.9 %collective-permute-start.18 = (bf16[2,2,128,256]{3,2,1,0:T(8,128)(2,1)S(1)}, bf16[2,2,128,256]{3,2,1,0:T(8,128)(2,1)S(1)}, u32[]{:S(2)}, u32[]{:S(2)}) collective-permute-start(bf16[2,2,128,256]{3,2,1,0:T(8,128)(2,1)S(1)} %get-tuple-element.72), channel_id=1, source_target_pairs={{0,4},{2,6},{4,0},{6,2},{8,12},{10,14},{12,8},{14,10},{16,20},{18,... | collective-permute-start | bytes 786440 | tf_op jit(solution)/shard_map/ppermute | solution.py:258
  134.0 1.3 collective-permute-start.15
  135.3 1.3 collective-permute-start.16
  136.6 3.5 %collective-permute-done.18.got_ref = bf16[2,2,128,256]{3,2,1,0:T(8,128)(2,1)S(1)} collective-permute-done((bf16[2,2,128,256]{3,2,1,0:T(8,128)(2,1)S(1)}, bf16[2,2,128,256]{3,2,1,0:T(8,128)(2,1)S(1)}, u32[]{:S(2)}, u32[]{:S(2)}) %collective-permute-start.18) | collective-permute-done | bytes 262176 | tf_op jit(solution)/shard_map/ppermute | solution.py:258
  140.2 1.3 collective-permute-start.20
  141.5 1.3 collective-permute-start.21
  142.8 2.7 %collective-permute-done.22.got_ref = bf16[2,2,128,256]{3,2,1,0:T(8,128)(2,1)S(1)} collective-permute-done((bf16[2,2,128,256]{3,2,1,0:T(8,128)(2,1)S(1)}, bf16[2,2,128,256]{3,2,1,0:T(8,128)(2,1)S(1)}, u32[]{:S(2)}, u32[]{:S(2)}) %collective-permute-start.22) | collective-permute-done | bytes 262176 | tf_op jit(solution)/shard_map/ppermute | solution.py:258
  145.6 1.3 collective-permute-start.24
  146.9 3.7 %collective-permute-done.15.refs_4_ = bf16[2,128,256]{2,1,0:T(8,128)(2,1)S(1)} collective-permute-done((bf16[2,128,256]{2,1,0:T(8,128)(2,1)S(1)}, bf16[2,128,256]{2,1,0:T(8,128)(2,1)S(1)}, u32[]{:S(2)}, u32[]{:S(2)}) %collective-permute-start.15) | collective-permute-done | bytes 131104 | tf_op jit(solution)/shard_map/ppermute | solution.py:254
  150.5 1.3 collective-permute-start.25
  151.8 9.0 %collective-permute-done.16.refs_5_ = bf16[2,128,256]{2,1,0:T(8,128)(2,1)S(1)} collective-permute-done((bf16[2,128,256]{2,1,0:T(8,128)(2,1)S(1)}, bf16[2,128,256]{2,1,0:T(8,128)(2,1)S(1)}, u32[]{:S(2)}, u32[]{:S(2)}) %collective-permute-start.16) | collective-permute-done | bytes 131104 | tf_op jit(solution)/shard_map/ppermute | solution.py:254
  160.8 8.9 %collective-permute-done.21.refs_8_ = bf16[2,128,256]{2,1,0:T(8,128)(2,1)S(1)} collective-permute-done((bf16[2,128,256]{2,1,0:T(8,128)(2,1)S(1)}, bf16[2,128,256]{2,1,0:T(8,128)(2,1)S(1)}, u32[]{:S(2)}, u32[]{:S(2)}) %collective-permute-start.21) | collective-permute-done | bytes 131104 | tf_op jit(solution)/shard_map/ppermute | solution.py:254
  170.0 1.6 collective-permute-start.23
  171.5 2.6 %collective-permute-done.25.refs_2_ = bf16[2,128,256]{2,1,0:T(8,128)(2,1)S(1)} collective-permute-done((bf16[2,128,256]{2,1,0:T(8,128)(2,1)S(1)}, bf16[2,128,256]{2,1,0:T(8,128)(2,1)S(1)}, u32[]{:S(2)}, u32[]{:S(2)}) %collective-permute-start.25) | collective-permute-done | bytes 131104 | tf_op jit(solution)/shard_map/ppermute | solution.py:254
  174.3 1.6 collective-permute-start.26
  176.1 2.6 %collective-permute-done.26 = bf16[1,2,128,128]{3,2,1,0:T(8,128)(2,1)S(1)} collective-permute-done((bf16[1,2,128,128]{3,2,1,0:T(8,128)(2,1)S(1)}, bf16[1,2,128,128]{3,2,1,0:T(8,128)(2,1)S(1)}, u32[]{:S(2)}, u32[]{:S(2)}) %collective-permute-start.26) | collective-permute-done | bytes 65568 | tf_op jit(solution)/shard_map/ppermute | solution.py:267
  (94 shorter events, 6.2 us)
Async XLA Ops:
  2.6 9.3 %collective-permute-start = (bf16[2,128,512]{2,1,0:T(8,128)(2,1)S(1)}, bf16[2,128,512]{2,1,0:T(8,128)(2,1)S(1)}, u32[]{:S(2)}, u32[]{:S(2)}) collective-permute-start(bf16[2,128,512]{2,1,0:T(8,128)(2,1)S(1)} %pack_for_tp.1), channel_id=1, source_target_pairs={{0,1},{1,0},{2,3},{3,2},{4,5},{5,4},{6,7},{7,6},{8,9},{9,8},{10,11... | collective-permute-start | bytes 786440 | tf_op jit(solution)/shard_map/ppermute | solution.py:267
  12.0 32.6 %copy-start.13 = (bf16[2,256,128]{2,1,0:T(8,128)(2,1)}, bf16[2,256,128]{2,1,0:T(8,128)(2,1)S(1)}, u32[]{:S(2)}) copy-start(bf16[2,256,128]{2,1,0:T(8,128)(2,1)S(1)} %get-tuple-element.44.own_ref) | copy-start | bytes 393220
  12.0 57.0 %copy-start.8 = (bf16[2,256,384]{2,1,0:T(8,128)(2,1)}, bf16[2,256,384]{2,1,0:T(8,128)(2,1)S(1)}, u32[]{:S(2)}) copy-start(bf16[2,256,384]{2,1,0:T(8,128)(2,1)S(1)} %get-tuple-element.43.own_ref) | copy-start | bytes 1179652
  12.0 7.2 %collective-permute-start.4 = (bf16[2,256,128]{2,1,0:T(8,128)(2,1)S(1)}, bf16[2,256,128]{2,1,0:T(8,128)(2,1)S(1)}, u32[]{:S(2)}, u32[]{:S(2)}) collective-permute-start(bf16[2,256,128]{2,1,0:T(8,128)(2,1)S(1)} %get-tuple-element.44.own_ref), channel_id=1, source_target_pairs={{0,8},{2,10},{4,12},{6,14},{8,16},{10,18},{12,20},{14,22},{16,24},... | collective-permute-start | bytes 393224 | tf_op jit(solution)/shard_map/ppermute | solution.py:254
  15.7 13.7 %collective-permute-start.1 = (bf16[2,256,384]{2,1,0:T(8,128)(2,1)S(1)}, bf16[2,256,384]{2,1,0:T(8,128)(2,1)S(1)}, u32[]{:S(2)}, u32[]{:S(2)}) collective-permute-start(bf16[2,256,384]{2,1,0:T(8,128)(2,1)S(1)} %get-tuple-element.43.own_ref), channel_id=1, source_target_pairs={{0,8},{2,10},{4,12},{6,14},{8,16},{10,18},{12,20},{14,22},{16,24},... | collective-permute-start | bytes 1179656 | tf_op jit(solution)/shard_map/ppermute | solution.py:254
  19.2 25.4 %copy-start.14 = (bf16[2,256,128]{2,1,0:T(8,128)(2,1)}, bf16[2,256,128]{2,1,0:T(8,128)(2,1)S(1)}, u32[]{:S(2)}) copy-start(bf16[2,256,128]{2,1,0:T(8,128)(2,1)S(1)} %collective-permute-done.4.far_ref) | copy-start | bytes 393220
  19.2 10.2 %collective-permute-start.5 = (bf16[2,256,128]{2,1,0:T(8,128)(2,1)S(1)}, bf16[2,256,128]{2,1,0:T(8,128)(2,1)S(1)}, u32[]{:S(2)}, u32[]{:S(2)}) collective-permute-start(bf16[2,256,128]{2,1,0:T(8,128)(2,1)S(1)} %collective-permute-done.4.far_ref), channel_id=1, source_target_pairs={{0,8},{2,10},{4,12},{6,14},{8,16},{10,18},{12,20},{14,22},{16,24},... | collective-permute-start | bytes 393224 | tf_op jit(solution)/shard_map/ppermute | solution.py:254
  29.4 39.5 %copy-start.9 = (bf16[2,256,384]{2,1,0:T(8,128)(2,1)}, bf16[2,256,384]{2,1,0:T(8,128)(2,1)S(1)}, u32[]{:S(2)}) copy-start(bf16[2,256,384]{2,1,0:T(8,128)(2,1)S(1)} %collective-permute-done.1.far_ref) | copy-start | bytes 1179652
  29.5 19.3 %collective-permute-start.2 = (bf16[2,256,384]{2,1,0:T(8,128)(2,1)S(1)}, bf16[2,256,384]{2,1,0:T(8,128)(2,1)S(1)}, u32[]{:S(2)}, u32[]{:S(2)}) collective-permute-start(bf16[2,256,384]{2,1,0:T(8,128)(2,1)S(1)} %collective-permute-done.1.far_ref), channel_id=1, source_target_pairs={{0,8},{2,10},{4,12},{6,14},{8,16},{10,18},{12,20},{14,22},{16,24},... | collective-permute-start | bytes 1179656 | tf_op jit(solution)/shard_map/ppermute | solution.py:254
  33.9 6.4 %collective-permute-start.6 = (bf16[2,2,256,128]{3,2,1,0:T(8,128)(2,1)S(1)}, bf16[2,2,256,128]{3,2,1,0:T(8,128)(2,1)S(1)}, u32[]{:S(2)}, u32[]{:S(2)}) collective-permute-start(bf16[2,2,256,128]{3,2,1,0:T(8,128)(2,1)S(1)} %pad_maximum_fusion.1), channel_id=1, source_target_pairs={{0,4},{2,6},{4,0},{6,2},{8,12},{10,14},{12,8},{14,10},{16,20},{18,... | collective-permute-start | bytes 786440 | tf_op jit(solution)/shard_map/ppermute | solution.py:258
  40.3 4.3 %copy-start.15 = (bf16[2,2,256,128]{3,2,1,0:T(8,128)(2,1)}, bf16[2,2,256,128]{3,2,1,0:T(8,128)(2,1)S(1)}, u32[]{:S(2)}) copy-start(bf16[2,2,256,128]{3,2,1,0:T(8,128)(2,1)S(1)} %collective-permute-done.6.x_ref) | copy-start | bytes 786436
  40.4 10.1 %collective-permute-start.7 = (bf16[4,2,256,128]{3,2,1,0:T(8,128)(2,1)S(1)}, bf16[4,2,256,128]{3,2,1,0:T(8,128)(2,1)S(1)}, u32[]{:S(2)}, u32[]{:S(2)}) collective-permute-start(bf16[4,2,256,128]{3,2,1,0:T(8,128)(2,1)S(1)} %core_swap_0.1), channel_id=1, source_target_pairs={{0,2},{2,0},{4,6},{6,4},{8,10},{10,8},{12,14},{14,12},{16,18},{18,... | collective-permute-start | bytes 1572872 | tf_op jit(solution)/shard_map/ppermute | solution.py:258
  48.9 1.6 copy-start.20
  48.9 20.0 %collective-permute-start.3 = (bf16[2,2,256,384]{3,2,1,0:T(8,128)(2,1)S(1)}, bf16[2,2,256,384]{3,2,1,0:T(8,128)(2,1)S(1)}, u32[]{:S(2)}, u32[]{:S(2)}) collective-permute-start(bf16[2,2,256,384]{3,2,1,0:T(8,128)(2,1)S(1)} %pad_maximum_fusion.rest_0_), channel_id=1, source_target_pairs={{0,4},{2,6},{4,0},{6,2},{8,12},{10,14},{12,8},{14,10},{16,20},{18,... | collective-permute-start | bytes 2359304 | tf_op jit(solution)/shard_map/ppermute | solution.py:258
  68.9 5.0 %copy-start.12 = (bf16[2,2,256,384]{3,2,1,0:T(8,128)(2,1)}, bf16[2,2,256,384]{3,2,1,0:T(8,128)(2,1)S(1)}, u32[]{:S(2)}) copy-start(bf16[2,2,256,384]{3,2,1,0:T(8,128)(2,1)S(1)} %collective-permute-done.3.x_ref) | copy-start | bytes 2359300
  69.0 1.3 copy-start.3
  70.3 1.0 copy-start.24
  70.4 3.5 %collective-permute-start.8 = (bf16[4,2,256,384]{3,2,1,0:T(8,128)(2,1)S(1)}, bf16[4,2,256,384]{3,2,1,0:T(8,128)(2,1)S(1)}, u32[]{:S(2)}, u32[]{:S(2)}) collective-permute-start(bf16[4,2,256,384]{3,2,1,0:T(8,128)(2,1)S(1)} %core_swap_1.1), channel_id=1, source_target_pairs={{0,2},{2,0},{4,6},{6,4},{8,10},{10,8},{12,14},{14,12},{16,18},{18,... | collective-permute-start | bytes 4718600 | tf_op jit(solution)/shard_map/ppermute | solution.py:258
  71.3 12.7 %collective-permute-start.9 = (bf16[4,2,128,256]{3,2,1,0:T(8,128)(2,1)S(1)}, bf16[4,2,128,256]{3,2,1,0:T(8,128)(2,1)S(1)}, u32[]{:S(2)}, u32[]{:S(2)}) collective-permute-start(bf16[4,2,128,256]{3,2,1,0:T(8,128)(2,1)S(1)} %copy-done.24), channel_id=1, source_target_pairs={{0,2},{2,0},{4,6},{6,4},{8,10},{10,8},{12,14},{14,12},{16,18},{18,... | collective-permute-start | bytes 1572872 | tf_op jit(solution)/shard_map/ppermute | solution.py:258
  73.9 1.2 copy-start.23
  75.1 8.9 %copy-start.4 = (bf16[4,2,128,256]{3,2,1,0:T(8,128)(2,1)S(1)}, bf16[4,2,128,256]{3,2,1,0:T(8,128)(2,1)}, u32[]{:S(2)}) copy-start(bf16[4,2,128,256]{3,2,1,0:T(8,128)(2,1)} %get-tuple-element.45.refs_0_.even_ref) | copy-start | bytes 1572868
  84.0 1.0 copy-start.5
  85.2 4.8 %copy-start.19 = (bf16[2,2,128,256]{3,2,1,0:T(8,128)(2,1)}, bf16[2,2,128,256]{3,2,1,0:T(8,128)(2,1)S(1)}, u32[]{:S(2)}) copy-start(bf16[2,2,128,256]{3,2,1,0:T(8,128)(2,1)S(1)} %get-tuple-element.52.rest_2_) | copy-start | bytes 786436
  85.2 14.2 %collective-permute-start.11 = (bf16[2,2,128,256]{3,2,1,0:T(8,128)(2,1)S(1)}, bf16[2,2,128,256]{3,2,1,0:T(8,128)(2,1)S(1)}, u32[]{:S(2)}, u32[]{:S(2)}) collective-permute-start(bf16[2,2,128,256]{3,2,1,0:T(8,128)(2,1)S(1)} %get-tuple-element.52.rest_2_), channel_id=1, source_target_pairs={{0,4},{2,6},{4,0},{6,2},{8,12},{10,14},{12,8},{14,10},{16,20},{18,... | collective-permute-start | bytes 786440 | tf_op jit(solution)/shard_map/ppermute | solution.py:258
  90.0 13.1 %collective-permute-start.10 = (bf16[4,2,128,256]{3,2,1,0:T(8,128)(2,1)}, bf16[4,2,128,256]{3,2,1,0:T(8,128)(2,1)S(1)}, u32[]{:S(2)}, u32[]{:S(2)}) collective-permute-start(bf16[4,2,128,256]{3,2,1,0:T(8,128)(2,1)} %get-tuple-element.55), channel_id=1, source_target_pairs={{0,2},{2,0},{4,6},{6,4},{8,10},{10,8},{12,14},{14,12},{16,18},{18,... | collective-permute-start | bytes 1572872 | tf_op jit(solution)/shard_map/ppermute | solution.py:258
  90.0 13.1 %copy-start.6 = (bf16[4,2,128,256]{3,2,1,0:T(8,128)(2,1)S(1)}, bf16[4,2,128,256]{3,2,1,0:T(8,128)(2,1)}, u32[]{:S(2)}) copy-start(bf16[4,2,128,256]{3,2,1,0:T(8,128)(2,1)} %get-tuple-element.51.refs_0_.even_ref) | copy-start | bytes 1572868
  98.8 29.0 %collective-permute-start.17 = (bf16[4,2,128,256]{3,2,1,0:T(8,128)(2,1)}, bf16[4,2,128,256]{3,2,1,0:T(8,128)(2,1)S(1)}, u32[]{:S(2)}, u32[]{:S(2)}) collective-permute-start(bf16[4,2,128,256]{3,2,1,0:T(8,128)(2,1)} %get-tuple-element.69), channel_id=1, source_target_pairs={{0,2},{2,0},{4,6},{6,4},{8,10},{10,8},{12,14},{14,12},{16,18},{18,... | collective-permute-start | bytes 1572872 | tf_op jit(solution)/shard_map/ppermute | solution.py:258
  99.4 1.0 copy-start
  100.5 7.4 %copy-start.16 = (bf16[2,128,256]{2,1,0:T(8,128)(2,1)}, bf16[2,128,256]{2,1,0:T(8,128)(2,1)S(1)}, u32[]{:S(2)}) copy-start(bf16[2,128,256]{2,1,0:T(8,128)(2,1)S(1)} %get-tuple-element.59.rest_3_.refs_0_) | copy-start | bytes 393220
  100.5 20.4 %collective-permute-start.12 = (bf16[2,128,256]{2,1,0:T(8,128)(2,1)S(1)}, bf16[2,128,256]{2,1,0:T(8,128)(2,1)S(1)}, u32[]{:S(2)}, u32[]{:S(2)}) collective-permute-start(bf16[2,128,256]{2,1,0:T(8,128)(2,1)S(1)} %get-tuple-element.62), channel_id=1, source_target_pairs={{8,0},{10,2},{12,4},{14,6},{16,8},{18,10},{20,12},{22,14},{24,16},... | collective-permute-start | bytes 393224 | tf_op jit(solution)/shard_map/ppermute | solution.py:254
  101.8 25.9 %collective-permute-start.13 = (bf16[2,128,256]{2,1,0:T(8,128)(2,1)S(1)}, bf16[2,128,256]{2,1,0:T(8,128)(2,1)S(1)}, u32[]{:S(2)}, u32[]{:S(2)}) collective-permute-start(bf16[2,128,256]{2,1,0:T(8,128)(2,1)S(1)} %get-tuple-element.63), channel_id=1, source_target_pairs={{16,0},{18,2},{20,4},{22,6},{24,8},{26,10},{28,12},{30,14},{17,1},... | collective-permute-start | bytes 393224 | tf_op jit(solution)/shard_map/ppermute | solution.py:254
  103.2 1.0 copy-start.1
  104.4 3.5 %copy-start.18 = (bf16[2,2,128,256]{3,2,1,0:T(8,128)(2,1)}, bf16[2,2,128,256]{3,2,1,0:T(8,128)(2,1)S(1)}, u32[]{:S(2)}) copy-start(bf16[2,2,128,256]{3,2,1,0:T(8,128)(2,1)S(1)} %get-tuple-element.57.rest_2_) | copy-start | bytes 786436
  104.4 23.3 %collective-permute-start.14 = (bf16[2,2,128,256]{3,2,1,0:T(8,128)(2,1)S(1)}, bf16[2,2,128,256]{3,2,1,0:T(8,128)(2,1)S(1)}, u32[]{:S(2)}, u32[]{:S(2)}) collective-permute-start(bf16[2,2,128,256]{3,2,1,0:T(8,128)(2,1)S(1)} %get-tuple-element.57.rest_2_), channel_id=1, source_target_pairs={{0,4},{2,6},{4,0},{6,2},{8,12},{10,14},{12,8},{14,10},{16,20},{18,... | collective-permute-start | bytes 786440 | tf_op jit(solution)/shard_map/ppermute | solution.py:258
  107.9 20.0 %copy-start.2 = (bf16[4,2,128,256]{3,2,1,0:T(8,128)(2,1)S(1)}, bf16[4,2,128,256]{3,2,1,0:T(8,128)(2,1)}, u32[]{:S(2)}) copy-start(bf16[4,2,128,256]{3,2,1,0:T(8,128)(2,1)} %get-tuple-element.56.refs_0_.even_ref) | copy-start | bytes 1572868
  127.8 5.2 %collective-permute-start.19 = (bf16[4,2,128,256]{3,2,1,0:T(8,128)(2,1)}, bf16[4,2,128,256]{3,2,1,0:T(8,128)(2,1)S(1)}, u32[]{:S(2)}, u32[]{:S(2)}) collective-permute-start(bf16[4,2,128,256]{3,2,1,0:T(8,128)(2,1)} %get-tuple-element.73), channel_id=1, source_target_pairs={{0,2},{2,0},{4,6},{6,4},{8,10},{10,8},{12,14},{14,12},{16,18},{18,... | collective-permute-start | bytes 1572872 | tf_op jit(solution)/shard_map/ppermute | solution.py:258
  127.9 1.0 copy-start.7
  128.9 40.8 %copy-start.17 = (bf16[2,128,256]{2,1,0:T(8,128)(2,1)S(1)}, bf16[2,128,256]{2,1,0:T(8,128)(2,1)}, u32[]{:S(2)}) copy-start(bf16[2,128,256]{2,1,0:T(8,128)(2,1)} %copy-done.16) | copy-start | bytes 393220
  129.1 11.0 %collective-permute-start.18 = (bf16[2,2,128,256]{3,2,1,0:T(8,128)(2,1)S(1)}, bf16[2,2,128,256]{3,2,1,0:T(8,128)(2,1)S(1)}, u32[]{:S(2)}, u32[]{:S(2)}) collective-permute-start(bf16[2,2,128,256]{3,2,1,0:T(8,128)(2,1)S(1)} %get-tuple-element.72), channel_id=1, source_target_pairs={{0,4},{2,6},{4,0},{6,2},{8,12},{10,14},{12,8},{14,10},{16,20},{18,... | collective-permute-start | bytes 786440 | tf_op jit(solution)/shard_map/ppermute | solution.py:258
  133.1 12.4 %collective-permute-start.22 = (bf16[2,2,128,256]{3,2,1,0:T(8,128)(2,1)S(1)}, bf16[2,2,128,256]{3,2,1,0:T(8,128)(2,1)S(1)}, u32[]{:S(2)}, u32[]{:S(2)}) collective-permute-start(bf16[2,2,128,256]{3,2,1,0:T(8,128)(2,1)S(1)} %get-tuple-element.74.refs_0_), channel_id=1, source_target_pairs={{0,4},{2,6},{4,0},{6,2},{8,12},{10,14},{12,8},{14,10},{16,20},{18,... | collective-permute-start | bytes 786440 | tf_op jit(solution)/shard_map/ppermute | solution.py:258
  134.0 16.5 %collective-permute-start.15 = (bf16[2,128,256]{2,1,0:T(8,128)(2,1)S(1)}, bf16[2,128,256]{2,1,0:T(8,128)(2,1)S(1)}, u32[]{:S(2)}, u32[]{:S(2)}) collective-permute-start(bf16[2,128,256]{2,1,0:T(8,128)(2,1)S(1)} %get-tuple-element.67), channel_id=1, source_target_pairs={{8,0},{10,2},{12,4},{14,6},{16,8},{18,10},{20,12},{22,14},{24,16},... | collective-permute-start | bytes 393224 | tf_op jit(solution)/shard_map/ppermute | solution.py:254
  135.3 25.6 %collective-permute-start.16 = (bf16[2,128,256]{2,1,0:T(8,128)(2,1)S(1)}, bf16[2,128,256]{2,1,0:T(8,128)(2,1)S(1)}, u32[]{:S(2)}, u32[]{:S(2)}) collective-permute-start(bf16[2,128,256]{2,1,0:T(8,128)(2,1)S(1)} %get-tuple-element.68), channel_id=1, source_target_pairs={{16,0},{18,2},{20,4},{22,6},{24,8},{26,10},{28,12},{30,14},{17,1},... | collective-permute-start | bytes 393224 | tf_op jit(solution)/shard_map/ppermute | solution.py:254
  140.2 20.7 %collective-permute-start.20 = (bf16[2,128,256]{2,1,0:T(8,128)(2,1)S(1)}, bf16[2,128,256]{2,1,0:T(8,128)(2,1)S(1)}, u32[]{:S(2)}, u32[]{:S(2)}) collective-permute-start(bf16[2,128,256]{2,1,0:T(8,128)(2,1)S(1)} %get-tuple-element.76), channel_id=1, source_target_pairs={{8,0},{10,2},{12,4},{14,6},{16,8},{18,10},{20,12},{22,14},{24,16},... | collective-permute-start | bytes 393224 | tf_op jit(solution)/shard_map/ppermute | solution.py:254
  141.5 28.2 %collective-permute-start.21 = (bf16[2,128,256]{2,1,0:T(8,128)(2,1)S(1)}, bf16[2,128,256]{2,1,0:T(8,128)(2,1)S(1)}, u32[]{:S(2)}, u32[]{:S(2)}) collective-permute-start(bf16[2,128,256]{2,1,0:T(8,128)(2,1)S(1)} %get-tuple-element.77), channel_id=1, source_target_pairs={{16,0},{18,2},{20,4},{22,6},{24,8},{26,10},{28,12},{30,14},{17,1},... | collective-permute-start | bytes 393224 | tf_op jit(solution)/shard_map/ppermute | solution.py:254
  145.6 26.0 %collective-permute-start.24 = (bf16[2,128,256]{2,1,0:T(8,128)(2,1)S(1)}, bf16[2,128,256]{2,1,0:T(8,128)(2,1)S(1)}, u32[]{:S(2)}, u32[]{:S(2)}) collective-permute-start(bf16[2,128,256]{2,1,0:T(8,128)(2,1)S(1)} %get-tuple-element.80), channel_id=1, source_target_pairs={{8,0},{10,2},{12,4},{14,6},{16,8},{18,10},{20,12},{22,14},{24,16},... | collective-permute-start | bytes 393224 | tf_op jit(solution)/shard_map/ppermute | solution.py:254
  150.5 23.6 %collective-permute-start.25 = (bf16[2,128,256]{2,1,0:T(8,128)(2,1)S(1)}, bf16[2,128,256]{2,1,0:T(8,128)(2,1)S(1)}, u32[]{:S(2)}, u32[]{:S(2)}) collective-permute-start(bf16[2,128,256]{2,1,0:T(8,128)(2,1)S(1)} %get-tuple-element.81), channel_id=1, source_target_pairs={{16,0},{18,2},{20,4},{22,6},{24,8},{26,10},{28,12},{30,14},{17,1},... | collective-permute-start | bytes 393224 | tf_op jit(solution)/shard_map/ppermute | solution.py:254
  170.0 5.9 %collective-permute-start.23 = (bf16[3,2,128,128]{3,2,1,0:T(8,128)(2,1)S(1)}, bf16[3,2,128,128]{3,2,1,0:T(8,128)(2,1)S(1)}, u32[]{:S(2)}, u32[]{:S(2)}) collective-permute-start(bf16[3,2,128,128]{3,2,1,0:T(8,128)(2,1)S(1)} %constant_dynamic-slice_fusion.1), channel_id=1, source_target_pairs={{0,1},{1,0},{2,3},{3,2},{4,5},{5,4},{6,7},{7,6},{8,9},{9,8},{10,11... | collective-permute-start | bytes 589832 | tf_op jit(solution)/shard_map/ppermute | solution.py:267
  174.3 4.3 %collective-permute-start.26 = (bf16[1,2,128,128]{3,2,1,0:T(8,128)(2,1)S(1)}, bf16[1,2,128,128]{3,2,1,0:T(8,128)(2,1)S(1)}, u32[]{:S(2)}, u32[]{:S(2)}) collective-permute-start(bf16[1,2,128,128]{3,2,1,0:T(8,128)(2,1)S(1)} %constant_dynamic-slice_fusion), channel_id=1, source_target_pairs={{0,1},{1,0},{2,3},{3,2},{4,5},{5,4},{6,7},{7,6},{8,9},{9,8},{10,11... | collective-permute-start | bytes 196616 | tf_op jit(solution)/shard_map/ppermute | solution.py:267
  (5 other events, 4.2 us)
